TPU v7x, 512 devices: a whole 4x8x8 slice. The times are simulated.
512 devices in a mesh: dp: 16 (over x, y_hi, core), mp: 32 (over y_lo, z).
Axes of the slice: x: 4, y: 8 (y_hi: 2, y_lo: 4; y = y_hi * 4 + y_lo), z: 8, core: 2. Of those that a mesh axis runs over, the one named last changes fastest.
Arguments:
- tokens: bfloat16 [5120, 3072], P(('dp', 'mp')), parts along dimension 0, may hold values from -6 to 6
- w_input: bfloat16 [3072, 12288], P(None, 'mp'), may hold values from -0.109375 to 0.109375
- b_input: float32 [12288], P('mp'), may hold values from -3 to 3
- w_output: bfloat16 [12288, 3072], P('mp'), may hold values from -0.0546875 to 0.0546875
- b_output: float32 [3072], replicated, may hold values from -3 to 3
Outputs:
- mlp_out: float32 [5120, 3072], P(('dp', 'mp')), parts along dimension 0
There are 16 independent parts, one for each index of `dp`. A program takes and returns all parts, laid end to end along the dimension named above; an argument that names none is the same for every part. Nothing has to cross between parts.
All inputs are finite; a program needn't handle non-finite values.
Results may differ from a plain program's by a relative error of at most 0.0024.
Values may be sent and summed in bfloat16 or wider, within the bound.
No kernel may reach another device: no remote copies, remote signals or barrier semaphores. Data moves between devices by JAX's collectives and lax.ppermute only.
A program may use at most 64 MiB of HBM per device.

v0:
```python
import jax
import jax.numpy as jnp
from jax import lax
from jax.sharding import PartitionSpec as P


def body(tokens, w_input, b_input, w_output, b_output):
    gathered = lax.all_gather(tokens, "mp", axis=0, tiled=True)
    pre = jnp.dot(gathered, w_input, preferred_element_type=jnp.float32) + b_input
    hidden = jax.nn.gelu(pre, approximate=False).astype(jnp.bfloat16)
    partial_rows = jnp.dot(hidden, w_output, preferred_element_type=jnp.float32)
    summed = lax.psum_scatter(partial_rows, "mp", scatter_dimension=0, tiled=True)
    return summed + b_output


def solution(mesh):
    return jax.shard_map(
        body,
        mesh=mesh,
        in_specs=(P(("dp", "mp"), None), P(None, "mp"), P("mp"), P("mp", None), P()),
        out_specs=P(("dp", "mp"), None),
        check_vma=False,
    )
```

profile of v0, /device:TPU:6, one launch (start us, length us, event | category | flops | bytes accessed | tf_op | source)
XLA Modules:
  0.0 508.2 jit_solution(17499369157959714605)
XLA Ops:
  6.5 0.0 copy-start
  6.5 0.0 all-gather.3.cloned.1.call-start
  6.5 0.7 all-gather.3.cloned.1.call-update
  7.3 0.0 copy-start.2
  7.3 0.0 all-reduce.3.cloned.1.call-start
  7.3 164.4 %all-gather.3.cloned.1.call-done = bf16[32,10,3072]{2,1,0:T(8,128)(2,1)} async-done(((bf16[1,10,3072]{2,1,0:T(8,128)(2,1)}), bf16[32,10,3072]{2,1,0:T(8,128)(2,1)}) %all-gather.3.cloned.1.call-update) | async-done | bytes 1966096 | tf_op jit(solution)/shard_map/all_gather | solution.py:8
  171.8 4.3 reshape.3
  176.0 0.0 copy-done
  176.0 0.0 copy-done.2
  176.0 7.4 %fusion.10 = f32[320,3072]{1,0:T(8,128)} fusion(bf16[384,3072]{1,0:T(8,128)(2,1)S(1)} %copy-done, bf16[320,3072]{1,0:T(8,128)(2,1)} %reshape.3, bf16[3072,384]{1,0:T(8,128)(2,1)} %param.6, f32[384]{0:T(512)S(1)} %copy-done.2), kind=kOutput, calls=%fused_computation.20 | convolution fusion | flops 1518059520 | bytes 10618368 | tf_op jit(solution)/shard_map/dot_general | solution.py:11
  183.5 0.0 copy-start.1
  183.5 0.0 all-reduce.3.cloned.1.call-update
  183.5 1.3 dynamic-slice
  185.4 314.3 %all-reduce.3.cloned.1.call-done = f32[320,3072]{1,0:T(8,128)} async-done(((f32[320,3072]{1,0:T(8,128)}), f32[320,3072]{1,0:T(8,128)}) %all-reduce.3.cloned.1.call-update) | async-done | bytes 3932176
  499.7 0.0 copy-done.1
  499.7 1.7 dynamic-slice_add_fusion
Async XLA Ops:
  6.5 169.5 %copy-start = (bf16[384,3072]{1,0:T(8,128)(2,1)S(1)}, bf16[384,3072]{1,0:T(8,128)(2,1)}, u32[]{:S(2)}) copy-start(bf16[384,3072]{1,0:T(8,128)(2,1)} %param.8) | copy-start | bytes 7077892
  6.5 165.2 %all-gather.3.cloned.1.call-start = ((), (), s32[]{:S(2)}) async-start(), calls=%async_computation | async-start | bytes 3244032 | tf_op jit(solution)/shard_map/all_gather | solution.py:8
  7.3 168.8 %copy-start.2 = (f32[384]{0:T(512)S(1)}, f32[384]{0:T(512)}, u32[]{:S(2)}) copy-start(f32[384]{0:T(512)} %param.7) | copy-start | bytes 4612
  7.3 492.5 %all-reduce.3.cloned.1.call-start = ((), (), s32[]{:S(2)}) async-start(), calls=%async_computation.1 | async-start | bytes 7864320
  183.5 316.3 %copy-start.1 = (f32[3072]{0:T(1024)S(1)}, f32[3072]{0:T(1024)}, u32[]{:S(2)}) copy-start(f32[3072]{0:T(1024)} %param.9) | copy-start | bytes 36868
Sparse Core Ops, SparseCore 0:
  9.4 162.2 all-gather.2
  183.6 316.0 all-reduce.2
where the time goes:
time: 509 us; the launch traced here: 508 us
  waiting for transfers between devices  479 us (94%)
  between operations  14.1 us (3%)
  matrix products  7.44 us (1%)
  local copies, waits for them, and re-layouts  5.56 us (1%)
    unnamed x3, waiting for transfers between devices  315 us
    all_gather x1, waiting for transfers between devices, body(): gathered = lax.all_gather(tokens, 'mp', axis=0, tiled=True)  164 us
  transfers between devices with their start and end apart: 2, of which 2 were waited for; matrix products, arithmetic and copies ran while one was open for 0% of the time, Pallas kernels for 0%

commit v1 on v0

v1 whole, which is shorter than its diff:
```python
import jax
import jax.numpy as jnp
from jax import lax
from jax.sharding import Mesh, PartitionSpec as P

X, YH, CORES, YL, Z = 4, 2, 2, 4, 8
Y = YH * YL
NAMES = ("x", "y_hi", "core", "y_lo", "z")


def pairs(step):
    out = []
    for i in range(X * Y * CORES * Z):
        rest, z = divmod(i, Z)
        rest, yl = divmod(rest, YL)
        rest, core = divmod(rest, CORES)
        x, yh = divmod(rest, YH)
        x2, y2, c2, z2 = step(x, yh * YL + yl, core, z)
        yh2, yl2 = divmod(y2 % Y, YL)
        out.append((i, (((x2 * YH + yh2) * CORES + c2) * YL + yl2) * Z + z2 % Z))
    return out


def along_y(k):
    return pairs(lambda x, y, c, z: (x, y + k * (1 - 2 * c), c, z))


def body(tokens, w_input, b_input, w_output, b_output):
    rows = tokens.shape[0]
    mine = lax.all_gather(tokens, "z", axis=0, tiled=True)

    def mlp(block):
        pre = jnp.dot(block, w_input, preferred_element_type=jnp.float32) + b_input
        hidden = jax.nn.gelu(pre, approximate=False).astype(jnp.bfloat16)
        return jnp.dot(hidden, w_output, preferred_element_type=jnp.float32)

    hops = (2, 1, -1)
    away = [lax.ppermute(mine, NAMES, along_y(k)) for k in hops]
    total = mlp(mine)
    back = [
        lax.ppermute(mlp(block).astype(jnp.bfloat16), NAMES, along_y(-k))
        for block, k in zip(away, hops)
    ]
    for part in back:
        total = total + part.astype(jnp.float32)
    total = total.reshape(Z, rows, -1)
    me = lax.axis_index("z")
    own = lax.dynamic_index_in_dim(total, me, 0, keepdims=True)
    got = lax.all_to_all(total.astype(jnp.bfloat16), "z", 0, 0, tiled=True)
    at = lax.broadcasted_iota(jnp.int32, (Z, 1, 1), 0)
    summed = jnp.where(at == me, own, got.astype(jnp.float32)).sum(0)
    return summed + b_output


def solution(mesh):
    fine = Mesh(mesh.devices.reshape(X, YH, CORES, YL, Z), NAMES)
    mp = ("y_lo", "z")
    return jax.shard_map(
        body,
        mesh=fine,
        in_specs=(P(NAMES, None), P(None, mp), P(mp), P(mp, None), P()),
        out_specs=P(NAMES, None),
        check_vma=False,
    )
```

time: 509 us -> 123 us (0.24)
  waiting for transfers between devices: 479 us -> 38.4 us
  blocking collectives: 0 us -> 32.8 us
  starting transfers between devices: 0.04 us -> 26.7 us
  between operations: 14.1 us -> 0.1 us
  matrix products: 7.44 us -> 15.2 us
    unnamed x3 -> x0, waiting for transfers between devices: 315 us -> none
    all_gather x1 -> x0, waiting for transfers between devices: 164 us -> none  [body(): gathered = lax.all_gather(tokens, 'mp', axis=0, tiled=True)]
    all_gather x0 -> x1, blocking collectives: none -> 32.8 us  [body(): mine = lax.all_gather(tokens, 'z', axis=0, tiled=True)]
    ppermute x0 -> x6, waiting for transfers between devices: none -> 23.2 us  [the longest x3 18.4 us: body(): away = [lax.ppermute(mine, NAMES, along_y(k)) for k in hops]]
    ppermute x0 -> x6, starting transfers between devices: none -> 21.9 us  [the longest x3 11.7 us: body(): away = [lax.ppermute(mine, NAMES, along_y(k)) for k in hops]]
    all_to_all x0 -> x1, waiting for transfers between devices: none -> 15.2 us  [body(): got = lax.all_to_all(total.astype(jnp.bfloat16), 'z', 0, 0, tiled=True)]
    dot_general x1 -> x4, matrix products: 7.44 us -> 15.2 us  [mlp(): return jnp.dot(hidden, w_output, preferred_element_type=jnp.float32)]
  transfers between devices with their start and end apart: 2 -> 7, of which waited for: 2 -> 4; matrix products, arithmetic and copies ran while one was open for 0% -> 13% of each run, Pallas kernels for 0% -> 0%
where the time goes in v1:
time: 123 us; the launch traced here: 122 us
  waiting for transfers between devices  38.4 us (31%)
  blocking collectives  32.8 us (27%)
  starting transfers between devices  26.7 us (22%)
  matrix products  15.2 us (12%)
  other arithmetic  5.18 us (4%)
  local copies, waits for them, and re-layouts  4.01 us (3%)
    all_gather x1, blocking collectives, body(): mine = lax.all_gather(tokens, 'z', axis=0, tiled=True)  32.8 us
    ppermute x3, waiting for transfers between devices, body(): away = [lax.ppermute(mine, NAMES, along_y(k)) for k in hops]  18.4 us
    all_to_all x1, waiting for transfers between devices, body(): got = lax.all_to_all(total.astype(jnp.bfloat16), 'z', 0, 0, tiled=True)  15.2 us
    dot_general x4, matrix products, mlp(): return jnp.dot(hidden, w_output, preferred_element_type=jnp.float32)  15.2 us
    ppermute x3, starting transfers between devices, body(): away = [lax.ppermute(mine, NAMES, along_y(k)) for k in hops]  11.7 us
    ppermute x3, starting transfers between devices, body(): lax.ppermute(mlp(block).astype(jnp.bfloat16), NAMES, along_y(-k))  10.2 us
    all_to_all x1, starting transfers between devices, body(): got = lax.all_to_all(total.astype(jnp.bfloat16), 'z', 0, 0, tiled=True)  4.81 us
    ppermute x3, waiting for transfers between devices, body(): lax.ppermute(mlp(block).astype(jnp.bfloat16), NAMES, along_y(-k))  4.78 us
  transfers between devices with their start and end apart: 7, of which 4 were waited for; matrix products, arithmetic and copies ran while one was open for 13% of the time, Pallas kernels for 0%

profile of v1, /device:TPU:6, one launch (start us, length us, event | category | flops | bytes accessed | tf_op | source)
XLA Modules:
  0.0 122.3 jit_solution(14529035378137935278)
XLA Ops:
  0.0 32.8 %all-gather = bf16[8,10,3072]{2,1,0:T(8,128)(2,1)S(1)} all-gather(bf16[1,10,3072]{2,1,0:T(8,128)(2,1)} %bitcast.15), channel_id=1, replica_groups=mesh['x'=4,'y_hi'=2,'core'=2,'y_lo'=4,'z'=8] {'z'}, dimensions={0}, use_global_device_ids=true | all-gather | bytes 552960 | tf_op jit(solution)/shard_map/all_gather | solution.py:30
  32.8 1.0 reshape.12
  33.8 4.6 %collective-permute-start = (bf16[80,3072]{1,0:T(8,128)(2,1)}, bf16[80,3072]{1,0:T(8,128)(2,1)S(1)}, u32[]{:S(2)}, u32[]{:S(2)}) collective-permute-start(bf16[80,3072]{1,0:T(8,128)(2,1)} %reshape.12), channel_id=1, source_target_pairs={{0,16},{1,17},{2,18},{3,19},{4,20},{5,21},{6,22},{7,23},{8,24},{9,... | collective-permute-start | bytes 1474568 | tf_op jit(solution)/shard_map/ppermute | solution.py:38
  38.4 3.5 %collective-permute-start.2 = (bf16[80,3072]{1,0:T(8,128)(2,1)}, bf16[80,3072]{1,0:T(8,128)(2,1)S(1)}, u32[]{:S(2)}, u32[]{:S(2)}) collective-permute-start(bf16[80,3072]{1,0:T(8,128)(2,1)} %reshape.12), channel_id=1, source_target_pairs={{0,8},{1,9},{2,10},{3,11},{4,12},{5,13},{6,14},{7,15},{8,16},{9,17... | collective-permute-start | bytes 1474568 | tf_op jit(solution)/shard_map/ppermute | solution.py:38
  41.9 3.6 %collective-permute-start.4 = (bf16[80,3072]{1,0:T(8,128)(2,1)}, bf16[80,3072]{1,0:T(8,128)(2,1)}, u32[]{:S(2)}, u32[]{:S(2)}) collective-permute-start(bf16[80,3072]{1,0:T(8,128)(2,1)} %reshape.12), channel_id=1, source_target_pairs={{0,88},{1,89},{2,90},{3,91},{4,92},{5,93},{6,94},{7,95},{8,0},{9,1... | collective-permute-start | bytes 1474568 | tf_op jit(solution)/shard_map/ppermute | solution.py:38
  45.5 9.9 %collective-permute-done = bf16[80,3072]{1,0:T(8,128)(2,1)S(1)} collective-permute-done((bf16[80,3072]{1,0:T(8,128)(2,1)}, bf16[80,3072]{1,0:T(8,128)(2,1)S(1)}, u32[]{:S(2)}, u32[]{:S(2)}) %collective-permute-start) | collective-permute-done | bytes 491552 | tf_op jit(solution)/shard_map/ppermute | solution.py:38
  55.4 3.7 %convolution_convert_fusion.2 = bf16[80,3072]{1,0:T(8,128)(2,1)} fusion(bf16[384,3072]{1,0:T(8,128)(2,1)S(1)} %copy-done, bf16[80,3072]{1,0:T(8,128)(2,1)S(1)} %collective-permute-done, bf16[3072,384]{1,0:T(8,128)(2,1)} %param.6, f32[384]{0:T(512)} %param.7), kind=kOutput, calls=%fused_computation.2 | convolution fusion | flops 379760640 | bytes 5703168 | tf_op jit(solution)/shard_map/dot_general | solution.py:35
  59.1 4.2 %collective-permute-start.1 = (bf16[80,3072]{1,0:T(8,128)(2,1)}, bf16[80,3072]{1,0:T(8,128)(2,1)S(1)}, u32[]{:S(2)}, u32[]{:S(2)}) collective-permute-start(bf16[80,3072]{1,0:T(8,128)(2,1)} %convolution_convert_fusion.2), channel_id=1, source_target_pairs={{0,80},{1,81},{2,82},{3,83},{4,84},{5,85},{6,86},{7,87},{8,88},{9,... | collective-permute-start | bytes 1474568 | tf_op jit(solution)/shard_map/ppermute | solution.py:41
  63.3 8.5 %collective-permute-done.2 = bf16[80,3072]{1,0:T(8,128)(2,1)S(1)} collective-permute-done((bf16[80,3072]{1,0:T(8,128)(2,1)}, bf16[80,3072]{1,0:T(8,128)(2,1)S(1)}, u32[]{:S(2)}, u32[]{:S(2)}) %collective-permute-start.2) | collective-permute-done | bytes 491552 | tf_op jit(solution)/shard_map/ppermute | solution.py:38
  71.9 3.7 %convolution_convert_fusion.1 = bf16[80,3072]{1,0:T(8,128)(2,1)} fusion(bf16[384,3072]{1,0:T(8,128)(2,1)S(1)} %copy-done, bf16[80,3072]{1,0:T(8,128)(2,1)S(1)} %collective-permute-done.2, bf16[3072,384]{1,0:T(8,128)(2,1)} %param.6, f32[384]{0:T(512)S(1)} %copy-done.4), kind=kOutput, calls=%fused_computation.1 | convolution fusion | flops 379760640 | bytes 5703168 | tf_op jit(solution)/shard_map/dot_general | solution.py:35
  75.6 3.2 %collective-permute-start.3 = (bf16[80,3072]{1,0:T(8,128)(2,1)}, bf16[80,3072]{1,0:T(8,128)(2,1)}, u32[]{:S(2)}, u32[]{:S(2)}) collective-permute-start(bf16[80,3072]{1,0:T(8,128)(2,1)} %convolution_convert_fusion.1), channel_id=1, source_target_pairs={{0,88},{1,89},{2,90},{3,91},{4,92},{5,93},{6,94},{7,95},{8,0},{9,1... | collective-permute-start | bytes 1474568 | tf_op jit(solution)/shard_map/ppermute | solution.py:41
  78.8 3.9 %convolution_convert_fusion = bf16[80,3072]{1,0:T(8,128)(2,1)} fusion(bf16[384,3072]{1,0:T(8,128)(2,1)S(1)} %copy-done, bf16[80,3072]{1,0:T(8,128)(2,1)} %collective-permute-done.4, bf16[3072,384]{1,0:T(8,128)(2,1)} %param.6, f32[384]{0:T(512)S(1)} %copy-done.4), kind=kOutput, calls=%fused_computation | convolution fusion | flops 379760640 | bytes 5703168 | tf_op jit(solution)/shard_map/dot_general | solution.py:35
  82.7 2.8 %collective-permute-start.5 = (bf16[80,3072]{1,0:T(8,128)(2,1)}, bf16[80,3072]{1,0:T(8,128)(2,1)}, u32[]{:S(2)}, u32[]{:S(2)}) collective-permute-start(bf16[80,3072]{1,0:T(8,128)(2,1)} %convolution_convert_fusion), channel_id=1, source_target_pairs={{0,8},{1,9},{2,10},{3,11},{4,12},{5,13},{6,14},{7,15},{8,16},{9,17... | collective-permute-start | bytes 1474568 | tf_op jit(solution)/shard_map/ppermute | solution.py:41
  85.4 3.9 %fusion.40 = f32[80,3072]{1,0:T(8,128)} fusion(bf16[384,3072]{1,0:T(8,128)(2,1)S(1)} %copy-done, bf16[80,3072]{1,0:T(8,128)(2,1)S(1)} %copy-done.1, bf16[3072,384]{1,0:T(8,128)(2,1)} %param.6, f32[384]{0:T(512)S(1)} %copy-done.4), kind=kOutput, calls=%fused_computation.86 | convolution fusion | flops 379514880 | bytes 6194688 | tf_op jit(solution)/shard_map/dot_general | solution.py:35
  89.3 0.8 copy-done.2
  90.1 4.8 %collective-permute-done.5 = bf16[80,3072]{1,0:T(8,128)(2,1)} collective-permute-done((bf16[80,3072]{1,0:T(8,128)(2,1)}, bf16[80,3072]{1,0:T(8,128)(2,1)}, u32[]{:S(2)}, u32[]{:S(2)}) %collective-permute-start.5) | collective-permute-done | bytes 491552 | tf_op jit(solution)/shard_map/ppermute | solution.py:41
  94.9 1.8 %convert_add_fusion = f32[80,3072]{1,0:T(8,128)S(1)} fusion(bf16[80,3072]{1,0:T(8,128)(2,1)} %collective-permute-done.5, bf16[80,3072]{1,0:T(8,128)(2,1)} %collective-permute-done.3, f32[80,3072]{1,0:T(8,128)} %fusion.40, bf16[80,3072]{1,0:T(8,128)(2,1)} %copy-done.2), kind=kLoop, calls=%fused_computation.8 | loop fusion | flops 1474560 | bytes 3440640 | tf_op jit(solution)/shard_map/add | solution.py:45
  96.7 1.3 %reshape.10 = f32[8,10,3072]{2,1,0:T(8,128)} reshape(f32[80,3072]{1,0:T(8,128)S(1)} %convert_add_fusion) | data formatting | bytes 1966080 | tf_op jit(solution)/shard_map/reshape | solution.py:46
  98.0 2.4 %convert_element_type.46 = bf16[8,10,3072]{2,1,0:T(8,128)(2,1)} convert(f32[8,10,3072]{2,1,0:T(8,128)} %reshape.10) | non-fusion elementwise | flops 245760 | bytes 1474560 | tf_op jit(solution)/shard_map/convert_element_type | solution.py:49
  100.4 4.8 %all-to-all-start = ((bf16[8,10,3072]{2,1,0:T(8,128)(2,1)}), bf16[8,10,3072]{2,1,0:T(8,128)(2,1)S(1)}, u32[]{:S(2)}, u32[]{:S(2)}) async-start(bf16[8,10,3072]{2,1,0:T(8,128)(2,1)} %convert_element_type.46), calls=%async_computation | async-start | bytes 1572864 | tf_op jit(solution)/shard_map/all_to_all | solution.py:49
  105.2 0.9 dynamic-slice_bitcast_fusion
  106.2 15.2 %all-to-all-done = bf16[8,10,3072]{2,1,0:T(8,128)(2,1)S(1)} async-done(((bf16[8,10,3072]{2,1,0:T(8,128)(2,1)}), bf16[8,10,3072]{2,1,0:T(8,128)(2,1)S(1)}, u32[]{:S(2)}, u32[]{:S(2)}) %all-to-all-start) | async-done | bytes 491552 | tf_op jit(solution)/shard_map/all_to_all | solution.py:49
  121.4 0.3 select_reduce_fusion
  121.6 0.7 broadcast_add_fusion
  (13 shorter events, 0.0 us)
Async XLA Ops:
  0.0 55.4 %copy-start = (bf16[384,3072]{1,0:T(8,128)(2,1)S(1)}, bf16[384,3072]{1,0:T(8,128)(2,1)}, u32[]{:S(2)}) copy-start(bf16[384,3072]{1,0:T(8,128)(2,1)} %param.8) | copy-start | bytes 7077892
  33.8 38.1 %copy-start.4 = (f32[384]{0:T(512)S(1)}, f32[384]{0:T(512)}, u32[]{:S(2)}) copy-start(f32[384]{0:T(512)} %param.7) | copy-start | bytes 4612
  33.8 21.6 %collective-permute-start = (bf16[80,3072]{1,0:T(8,128)(2,1)}, bf16[80,3072]{1,0:T(8,128)(2,1)S(1)}, u32[]{:S(2)}, u32[]{:S(2)}) collective-permute-start(bf16[80,3072]{1,0:T(8,128)(2,1)} %reshape.12), channel_id=1, source_target_pairs={{0,16},{1,17},{2,18},{3,19},{4,20},{5,21},{6,22},{7,23},{8,24},{9,... | collective-permute-start | bytes 1474568 | tf_op jit(solution)/shard_map/ppermute | solution.py:38
  38.4 33.4 %collective-permute-start.2 = (bf16[80,3072]{1,0:T(8,128)(2,1)}, bf16[80,3072]{1,0:T(8,128)(2,1)S(1)}, u32[]{:S(2)}, u32[]{:S(2)}) collective-permute-start(bf16[80,3072]{1,0:T(8,128)(2,1)} %reshape.12), channel_id=1, source_target_pairs={{0,8},{1,9},{2,10},{3,11},{4,12},{5,13},{6,14},{7,15},{8,16},{9,17... | collective-permute-start | bytes 1474568 | tf_op jit(solution)/shard_map/ppermute | solution.py:38
  41.9 36.8 %collective-permute-start.4 = (bf16[80,3072]{1,0:T(8,128)(2,1)}, bf16[80,3072]{1,0:T(8,128)(2,1)}, u32[]{:S(2)}, u32[]{:S(2)}) collective-permute-start(bf16[80,3072]{1,0:T(8,128)(2,1)} %reshape.12), channel_id=1, source_target_pairs={{0,88},{1,89},{2,90},{3,91},{4,92},{5,93},{6,94},{7,95},{8,0},{9,1... | collective-permute-start | bytes 1474568 | tf_op jit(solution)/shard_map/ppermute | solution.py:38
  59.1 30.2 %collective-permute-start.1 = (bf16[80,3072]{1,0:T(8,128)(2,1)}, bf16[80,3072]{1,0:T(8,128)(2,1)S(1)}, u32[]{:S(2)}, u32[]{:S(2)}) collective-permute-start(bf16[80,3072]{1,0:T(8,128)(2,1)} %convolution_convert_fusion.2), channel_id=1, source_target_pairs={{0,80},{1,81},{2,82},{3,83},{4,84},{5,85},{6,86},{7,87},{8,88},{9,... | collective-permute-start | bytes 1474568 | tf_op jit(solution)/shard_map/ppermute | solution.py:41
  75.6 9.9 %copy-start.1 = (bf16[80,3072]{1,0:T(8,128)(2,1)S(1)}, bf16[80,3072]{1,0:T(8,128)(2,1)}, u32[]{:S(2)}) copy-start(bf16[80,3072]{1,0:T(8,128)(2,1)} %reshape.12) | copy-start | bytes 1474564
  75.6 13.8 %collective-permute-start.3 = (bf16[80,3072]{1,0:T(8,128)(2,1)}, bf16[80,3072]{1,0:T(8,128)(2,1)}, u32[]{:S(2)}, u32[]{:S(2)}) collective-permute-start(bf16[80,3072]{1,0:T(8,128)(2,1)} %convolution_convert_fusion.1), channel_id=1, source_target_pairs={{0,88},{1,89},{2,90},{3,91},{4,92},{5,93},{6,94},{7,95},{8,0},{9,1... | collective-permute-start | bytes 1474568 | tf_op jit(solution)/shard_map/ppermute | solution.py:41
  82.7 12.2 %collective-permute-start.5 = (bf16[80,3072]{1,0:T(8,128)(2,1)}, bf16[80,3072]{1,0:T(8,128)(2,1)}, u32[]{:S(2)}, u32[]{:S(2)}) collective-permute-start(bf16[80,3072]{1,0:T(8,128)(2,1)} %convolution_convert_fusion), channel_id=1, source_target_pairs={{0,8},{1,9},{2,10},{3,11},{4,12},{5,13},{6,14},{7,15},{8,16},{9,17... | collective-permute-start | bytes 1474568 | tf_op jit(solution)/shard_map/ppermute | solution.py:41
  89.3 0.8 copy-start.2
  98.0 23.6 %copy-start.3 = (f32[3072]{0:T(1024)S(1)}, f32[3072]{0:T(1024)}, u32[]{:S(2)}) copy-start(f32[3072]{0:T(1024)} %param.9) | copy-start | bytes 36868
  100.4 21.0 %all-to-all-start = ((bf16[8,10,3072]{2,1,0:T(8,128)(2,1)}), bf16[8,10,3072]{2,1,0:T(8,128)(2,1)S(1)}, u32[]{:S(2)}, u32[]{:S(2)}) async-start(bf16[8,10,3072]{2,1,0:T(8,128)(2,1)} %convert_element_type.46), calls=%async_computation | async-start | bytes 1572864 | tf_op jit(solution)/shard_map/all_to_all | solution.py:49

commit v2 on v1

v2 whole, which is shorter than its diff:
```python
import jax
import jax.numpy as jnp
from jax import lax
from jax.experimental import pallas as pl
from jax.experimental.pallas import tpu as pltpu
from jax.sharding import Mesh, PartitionSpec as P

X, YH, CORES, YL, Z = 4, 2, 2, 4, 8
Y = YH * YL
NAMES = ("x", "y_hi", "core", "y_lo", "z")

EIGHT, REST, QUARTERS = 8, 2, 4
MAIN, LEFT = EIGHT * Z, REST * Z


def pairs(step):
    out = []
    for i in range(X * Y * CORES * Z):
        rest, z = divmod(i, Z)
        rest, yl = divmod(rest, YL)
        rest, core = divmod(rest, CORES)
        x, yh = divmod(rest, YH)
        x2, y2, c2, z2 = step(x, yh * YL + yl, core, z)
        yh2, yl2 = divmod(y2 % Y, YL)
        out.append((i, (((x2 * YH + yh2) * CORES + c2) * YL + yl2) * Z + z2 % Z))
    return out


def along_y(block, k):
    return lax.ppermute(block, NAMES, pairs(lambda x, y, c, z: (x, y + k * (1 - 2 * c), c, z)))


def exchange_z(blocks):
    return lax.all_to_all(blocks.reshape(Z, EIGHT, -1), "z", 0, 0, tiled=True).reshape(MAIN, -1)


def picks(q):
    row = lax.broadcasted_iota(jnp.int32, (LEFT, MAIN), 0)
    col = lax.broadcasted_iota(jnp.int32, (LEFT, MAIN), 1)
    return (col == QUARTERS * row + q).astype(jnp.bfloat16)


def puts(q):
    row = lax.broadcasted_iota(jnp.int32, (MAIN, LEFT), 0)
    col = lax.broadcasted_iota(jnp.int32, (MAIN, LEFT), 1)
    return (row == QUARTERS * col + q).astype(jnp.bfloat16)


def dot(a, b):
    return jnp.dot(a, b, preferred_element_type=jnp.float32)


def copies_kernel(tokens, out):
    features = tokens.shape[1]
    part = features // QUARTERS
    rows = tokens[...].astype(jnp.float32)
    rest = [
        rows[EIGHT + r : EIGHT + r + 1, q * part : (q + 1) * part] for r in range(REST) for q in range(QUARTERS)
    ]
    out[:, :features] = jnp.concatenate([rows[:EIGHT]] * Z, 0).astype(jnp.bfloat16)
    out[:, features:] = jnp.concatenate(rest * Z, 0).astype(jnp.bfloat16)


def hidden_of(packed, w_input, b_input, block):
    features = w_input.shape[0]
    part = features // QUARTERS
    block[:MAIN] = packed[:, :features]
    left = packed[:, features:]
    for q in range(QUARTERS):
        block[MAIN:, q * part : (q + 1) * part] = dot(picks(q), left).astype(jnp.bfloat16)
    pre = dot(block[...], w_input[...]) + b_input[...]
    return (0.5 * pre * (1.0 + lax.erf(pre * (0.5**0.5)))).astype(jnp.bfloat16)


def away_kernel(packed, w_input, b_input, w_output, out, block):
    hidden = hidden_of(packed, w_input, b_input, block)
    features = w_output.shape[1]
    part = features // QUARTERS
    left = jnp.zeros((MAIN, part), jnp.float32)
    for q in range(QUARTERS):
        at = slice(q * part, (q + 1) * part)
        sums = dot(hidden, w_output[:, at])
        out[:, at] = sums[:MAIN].astype(jnp.bfloat16)
        left = left + dot(puts(q), sums[MAIN:].astype(jnp.bfloat16))
    out[:, features:] = left.astype(jnp.bfloat16)


def own_kernel(packed, w_input, b_input, w_output, out, block):
    hidden = hidden_of(packed, w_input, b_input, block)
    part = w_output.shape[1] // QUARTERS
    for q in range(QUARTERS):
        at = slice(q * part, (q + 1) * part)
        out[:, at] = dot(hidden, w_output[:, at])


def add_kernel(own, one, two, three, total, packed):
    features = own.shape[1]
    part = features // QUARTERS
    terms = (one, two, three)
    main = own[:MAIN]
    for term in terms:
        main = main + term[:, :features].astype(jnp.float32)
    total[:MAIN] = main
    packed[:, :features] = main.astype(jnp.bfloat16)
    left = jnp.zeros((MAIN, part), jnp.float32)
    for q in range(QUARTERS):
        at = slice(q * part, (q + 1) * part)
        sums = own[MAIN:, at]
        for term in terms:
            sums = sums + dot(picks(q), term[:, features:])
        total[MAIN:, at] = sums
        left = left + dot(puts(q), sums.astype(jnp.bfloat16))
    packed[:, features:] = left.astype(jnp.bfloat16)


def last_kernel(total, got, b_output, out):
    features = total.shape[1]
    part = features // QUARTERS
    me = lax.axis_index("z")
    bias = b_output[...]
    summed = jnp.zeros((EIGHT, got.shape[1]), jnp.float32)
    others = got[...].astype(jnp.float32)
    for z in range(Z):
        summed = summed + jnp.where(me == z, 0.0, others[z * EIGHT : (z + 1) * EIGHT])
    at = pl.multiple_of(me * EIGHT, EIGHT)
    out[:EIGHT] = summed[:, :features] + total[pl.ds(at, EIGHT)] + bias
    rows = lax.broadcasted_iota(jnp.int32, (LEFT, 1), 0)
    for r in range(REST):
        mine = jnp.where(rows == me * REST + r, total[MAIN:], 0.0).sum(0, keepdims=True) + bias
        for q in range(QUARTERS):
            cols = slice(q * part, (q + 1) * part)
            row = QUARTERS * r + q
            out[EIGHT + r : EIGHT + r + 1, cols] = mine[:, cols] + summed[row : row + 1, features:]


def call(kernel, outs, args, scratch=(), flops=0):
    moved = sum(a.size * a.dtype.itemsize for a in args) + sum(o.size * o.dtype.itemsize for o in outs)
    return pl.pallas_call(
        kernel,
        out_shape=outs,
        in_specs=[pl.BlockSpec(memory_space=pltpu.VMEM)] * len(args),
        out_specs=tuple(pl.BlockSpec(memory_space=pltpu.VMEM) for _ in outs),
        scratch_shapes=scratch,
        compiler_params=pltpu.CompilerParams(vmem_limit_bytes=32 << 20),
        cost_estimate=pl.CostEstimate(flops=flops, bytes_accessed=moved, transcendentals=0),
    )(*args)


def body(tokens, w_input, b_input, w_output, b_output):
    features, units = w_input.shape
    wide = features + features // QUARTERS
    rows = MAIN + LEFT
    weights = (w_input, b_input.reshape(1, -1), w_output)
    packed = jax.ShapeDtypeStruct((MAIN, wide), jnp.bfloat16)
    sums = jax.ShapeDtypeStruct((rows, features), jnp.float32)
    block = (pltpu.VMEM((rows, features), jnp.bfloat16),)
    flops = 4 * rows * features * units

    (copies,) = call(copies_kernel, (packed,), (tokens,))
    mine = exchange_z(copies)
    up1 = along_y(mine, 1)
    (own,) = call(own_kernel, (sums,), (mine,) + weights, block, flops)
    up2 = along_y(up1, 1)
    down1 = along_y(mine, -1)
    back = []
    for away, k in ((up1, -1), (down1, 1), (up2, -2)):
        (part,) = call(away_kernel, (packed,), (away,) + weights, block, flops)
        back.append(along_y(part, k))
    total, outgoing = call(add_kernel, (sums, packed), (own, *back))
    got = exchange_z(outgoing)
    (out,) = call(
        last_kernel,
        (jax.ShapeDtypeStruct((EIGHT + REST, features), jnp.float32),),
        (total, got, b_output.reshape(1, -1)),
    )
    return out


def solution(mesh):
    fine = Mesh(mesh.devices.reshape(X, YH, CORES, YL, Z), NAMES)
    mp = ("y_lo", "z")
    return jax.shard_map(
        body,
        mesh=fine,
        in_specs=(P(NAMES, None), P(None, mp), P(mp), P(mp, None), P()),
        out_specs=P(NAMES, None),
        check_vma=False,
    )
```

time: 123 us -> 102 us (0.83)
  the two profiles are of different devices: /device:TPU:6 before, /device:TPU:43 now
where the time goes in v2:
time: 102 us; the launch traced here: 101 us
  blocking collectives  44.9 us (44%)
  waiting for transfers between devices  26.2 us (26%)
  starting transfers between devices  17.4 us (17%)
  Pallas kernels  7.8 us (8%)
  local copies, waits for them, and re-layouts  4.93 us (5%)
    all_to_all x2, blocking collectives, exchange_z(): lax.all_to_all(blocks.reshape(Z, EIGHT, -1), 'z', 0, 0, tiled=True)  44.9 us
    ppermute x6, waiting for transfers between devices, along_y(): lax.ppermute(block, NAMES, pairs(lambda x, y, c, z: (x, y + k * (1 - 2 *...  26.2 us
    ppermute x6, starting transfers between devices, along_y(): lax.ppermute(block, NAMES, pairs(lambda x, y, c, z: (x, y + k * (1 - 2 *...  17.4 us
    pallas_call x7, Pallas kernels, call(): pl.pallas_call(kernel, out_shape=outs, in_specs=[pl.BlockSpec(memory_spac...  7.8 us
    unnamed x12, local copies, waits for them, and re-layouts  4.24 us
  transfers between devices with their start and end apart: 6, of which 4 were waited for; matrix products, arithmetic and copies ran while one was open for 1% of the time, Pallas kernels for 6%

profile of v2, /device:TPU:43, one launch (start us, length us, event | category | flops | bytes accessed | tf_op | source)
XLA Modules:
  0.0 101.4 jit_solution(12373325971313509129)
XLA Ops:
  0.0 0.9 copy-done.4
  0.9 25.2 %all_to_all.10 = bf16[8,8,3840]{2,1,0:T(8,128)(2,1)S(1)} all-to-all(bf16[8,8,3840]{2,1,0:T(8,128)(2,1)S(1)} %bitcast.6), channel_id=1, replica_groups=mesh['x'=4,'y_hi'=2,'core'=2,'y_lo'=4,'z'=8] {'z'}, dimensions={0} | all-to-all | bytes 983040 | tf_op jit(solution)/shard_map/all_to_all | solution.py:34
  26.1 3.0 %collective-permute-start = (bf16[64,3840]{1,0:T(8,128)(2,1)S(1)}, bf16[64,3840]{1,0:T(8,128)(2,1)S(1)}, u32[]{:S(2)}, u32[]{:S(2)}) collective-permute-start(bf16[64,3840]{1,0:T(8,128)(2,1)S(1)} %bitcast.7), channel_id=1, source_target_pairs={{0,8},{1,9},{2,10},{3,11},{4,12},{5,13},{6,14},{7,15},{8,16},{9,17... | collective-permute-start | bytes 1474568 | tf_op jit(solution)/shard_map/ppermute | solution.py:30
  29.1 2.3 %collective-permute-start.2 = (bf16[64,3840]{1,0:T(8,128)(2,1)S(1)}, bf16[64,3840]{1,0:T(8,128)(2,1)S(1)}, u32[]{:S(2)}, u32[]{:S(2)}) collective-permute-start(bf16[64,3840]{1,0:T(8,128)(2,1)S(1)} %bitcast.8), channel_id=1, source_target_pairs={{0,88},{1,89},{2,90},{3,91},{4,92},{5,93},{6,94},{7,95},{8,0},{9,1... | collective-permute-start | bytes 1474568 | tf_op jit(solution)/shard_map/ppermute | solution.py:30
  31.4 4.6 %collective-permute-done.packed = bf16[64,3840]{1,0:T(8,128)(2,1)S(1)} collective-permute-done((bf16[64,3840]{1,0:T(8,128)(2,1)S(1)}, bf16[64,3840]{1,0:T(8,128)(2,1)S(1)}, u32[]{:S(2)}, u32[]{:S(2)}) %collective-permute-start) | collective-permute-done | bytes 491552 | tf_op jit(solution)/shard_map/ppermute | solution.py:30
  36.0 3.0 %collective-permute-start.4 = (bf16[64,3840]{1,0:T(8,128)(2,1)S(1)}, bf16[64,3840]{1,0:T(8,128)(2,1)S(1)}, u32[]{:S(2)}, u32[]{:S(2)}) collective-permute-start(bf16[64,3840]{1,0:T(8,128)(2,1)S(1)} %collective-permute-done.packed), channel_id=1, source_target_pairs={{0,8},{1,9},{2,10},{3,11},{4,12},{5,13},{6,14},{7,15},{8,16},{9,17... | collective-permute-start | bytes 1474568 | tf_op jit(solution)/shard_map/ppermute | solution.py:30
  39.0 0.7 reshape.20.b_input
  39.7 4.3 %collective-permute-done.2.packed = bf16[64,3840]{1,0:T(8,128)(2,1)S(1)} collective-permute-done((bf16[64,3840]{1,0:T(8,128)(2,1)S(1)}, bf16[64,3840]{1,0:T(8,128)(2,1)S(1)}, u32[]{:S(2)}, u32[]{:S(2)}) %collective-permute-start.2) | collective-permute-done | bytes 491552 | tf_op jit(solution)/shard_map/ppermute | solution.py:30
  44.0 1.7 %copy-done = bf16[3072,384]{1,0:T(8,128)(2,1)S(1)} copy-done((bf16[3072,384]{1,0:T(8,128)(2,1)S(1)}, bf16[3072,384]{1,0:T(8,128)(2,1)}, u32[]{:S(2)}) %copy-start) | copy-done | bytes 2359320
  45.6 1.7 %copy-done.2 = bf16[384,3072]{1,0:T(8,128)(2,1)S(1)} copy-done((bf16[384,3072]{1,0:T(8,128)(2,1)S(1)}, bf16[384,3072]{1,0:T(8,128)(2,1)}, u32[]{:S(2)}) %copy-start.2) | copy-done | bytes 2359320
  47.3 1.7 %shard_map.58 = bf16[64,3840]{1,0:T(8,128)(2,1)S(1)} custom-call(bf16[64,3840]{1,0:T(8,128)(2,1)S(1)} %collective-permute-done.2.packed, bf16[3072,384]{1,0:T(8,128)(2,1)S(1)} %copy-done, f32[1,384]{1,0:T(1,128)S(1)} %reshape.20.b_input, bf16[384,3072]{1,0:T(8,128)(2,1)S(1)} %copy-done.2), custom_call_target="tpu_custom_call" | custom-call | flops 377487360 | bytes 5703168 | tf_op jit(solution)/shard_map/pallas_call | solution.py:138
  48.9 2.8 %collective-permute-start.3 = (bf16[64,3840]{1,0:T(8,128)(2,1)S(1)}, bf16[64,3840]{1,0:T(8,128)(2,1)S(1)}, u32[]{:S(2)}, u32[]{:S(2)}) collective-permute-start(bf16[64,3840]{1,0:T(8,128)(2,1)S(1)} %shard_map.58), channel_id=1, source_target_pairs={{0,8},{1,9},{2,10},{3,11},{4,12},{5,13},{6,14},{7,15},{8,16},{9,17... | collective-permute-start | bytes 1474568 | tf_op jit(solution)/shard_map/ppermute | solution.py:30
  51.8 1.7 %shard_map.57 = bf16[64,3840]{1,0:T(8,128)(2,1)S(1)} custom-call(bf16[64,3840]{1,0:T(8,128)(2,1)S(1)} %collective-permute-done.packed, bf16[3072,384]{1,0:T(8,128)(2,1)S(1)} %copy-done, f32[1,384]{1,0:T(1,128)S(1)} %reshape.20.b_input, bf16[384,3072]{1,0:T(8,128)(2,1)S(1)} %copy-done.2), custom_call_target="tpu_custom_call" | custom-call | flops 377487360 | bytes 5703168 | tf_op jit(solution)/shard_map/pallas_call | solution.py:138
  53.4 0.0 copy-start.1
  53.5 0.0 copy-start.3
  53.5 2.7 %collective-permute-start.1 = (bf16[64,3840]{1,0:T(8,128)(2,1)S(1)}, bf16[64,3840]{1,0:T(8,128)(2,1)S(1)}, u32[]{:S(2)}, u32[]{:S(2)}) collective-permute-start(bf16[64,3840]{1,0:T(8,128)(2,1)S(1)} %shard_map.57), channel_id=1, source_target_pairs={{0,88},{1,89},{2,90},{3,91},{4,92},{5,93},{6,94},{7,95},{8,0},{9,1... | collective-permute-start | bytes 1474568 | tf_op jit(solution)/shard_map/ppermute | solution.py:30
  56.2 1.7 %shard_map.59 = bf16[64,3840]{1,0:T(8,128)(2,1)S(1)} custom-call(bf16[64,3840]{1,0:T(8,128)(2,1)S(1)} %collective-permute-done.4.packed, bf16[3072,384]{1,0:T(8,128)(2,1)S(1)} %copy-done, f32[1,384]{1,0:T(1,128)S(1)} %reshape.20.b_input, bf16[384,3072]{1,0:T(8,128)(2,1)S(1)} %copy-done.2), custom_call_target="tpu_custom_call" | custom-call | flops 377487360 | bytes 5703168 | tf_op jit(solution)/shard_map/pallas_call | solution.py:138
  57.9 3.6 %collective-permute-start.5 = (bf16[64,3840]{1,0:T(8,128)(2,1)S(1)}, bf16[64,3840]{1,0:T(8,128)(2,1)S(1)}, u32[]{:S(2)}, u32[]{:S(2)}) collective-permute-start(bf16[64,3840]{1,0:T(8,128)(2,1)S(1)} %shard_map.59), channel_id=1, source_target_pairs={{0,80},{1,81},{2,82},{3,83},{4,84},{5,85},{6,86},{7,87},{8,88},{9,... | collective-permute-start | bytes 1474568 | tf_op jit(solution)/shard_map/ppermute | solution.py:30
  61.5 1.2 %shard_map.56.own = f32[80,3072]{1,0:T(8,128)S(1)} custom-call(bf16[64,3840]{1,0:T(8,128)(2,1)S(1)} %bitcast.9, bf16[3072,384]{1,0:T(8,128)(2,1)S(1)} %copy-done.1, f32[1,384]{1,0:T(1,128)S(1)} %reshape.20.b_input, bf16[384,3072]{1,0:T(8,128)(2,1)S(1)} %copy-done.3), custom_call_target="tpu_custom_call" | custom-call | flops 377487360 | bytes 6194688 | tf_op jit(solution)/shard_map/pallas_call | solution.py:138
  62.7 5.5 %collective-permute-done.1.one = bf16[64,3840]{1,0:T(8,128)(2,1)S(1)} collective-permute-done((bf16[64,3840]{1,0:T(8,128)(2,1)S(1)}, bf16[64,3840]{1,0:T(8,128)(2,1)S(1)}, u32[]{:S(2)}, u32[]{:S(2)}) %collective-permute-start.1) | collective-permute-done | bytes 491552 | tf_op jit(solution)/shard_map/ppermute | solution.py:30
  68.2 11.8 %collective-permute-done.5.three = bf16[64,3840]{1,0:T(8,128)(2,1)S(1)} collective-permute-done((bf16[64,3840]{1,0:T(8,128)(2,1)S(1)}, bf16[64,3840]{1,0:T(8,128)(2,1)S(1)}, u32[]{:S(2)}, u32[]{:S(2)}) %collective-permute-start.5) | collective-permute-done | bytes 491552 | tf_op jit(solution)/shard_map/ppermute | solution.py:30
  80.0 0.8 shard_map.60
  80.8 19.7 %all_to_all.11 = bf16[8,8,3840]{2,1,0:T(8,128)(2,1)S(1)} all-to-all(bf16[8,8,3840]{2,1,0:T(8,128)(2,1)S(1)} %bitcast.10), channel_id=1, replica_groups=mesh['x'=4,'y_hi'=2,'core'=2,'y_lo'=4,'z'=8] {'z'}, dimensions={0} | all-to-all | bytes 983040 | tf_op jit(solution)/shard_map/all_to_all | solution.py:34
  100.5 0.9 shard_map.61
  (10 shorter events, 0.1 us)
Async XLA Ops:
  0.0 0.9 copy-start.4
  26.1 9.9 %collective-permute-start = (bf16[64,3840]{1,0:T(8,128)(2,1)S(1)}, bf16[64,3840]{1,0:T(8,128)(2,1)S(1)}, u32[]{:S(2)}, u32[]{:S(2)}) collective-permute-start(bf16[64,3840]{1,0:T(8,128)(2,1)S(1)} %bitcast.7), channel_id=1, source_target_pairs={{0,8},{1,9},{2,10},{3,11},{4,12},{5,13},{6,14},{7,15},{8,16},{9,17... | collective-permute-start | bytes 1474568 | tf_op jit(solution)/shard_map/ppermute | solution.py:30
  29.1 14.8 %collective-permute-start.2 = (bf16[64,3840]{1,0:T(8,128)(2,1)S(1)}, bf16[64,3840]{1,0:T(8,128)(2,1)S(1)}, u32[]{:S(2)}, u32[]{:S(2)}) collective-permute-start(bf16[64,3840]{1,0:T(8,128)(2,1)S(1)} %bitcast.8), channel_id=1, source_target_pairs={{0,88},{1,89},{2,90},{3,91},{4,92},{5,93},{6,94},{7,95},{8,0},{9,1... | collective-permute-start | bytes 1474568 | tf_op jit(solution)/shard_map/ppermute | solution.py:30
  36.0 20.2 %collective-permute-start.4 = (bf16[64,3840]{1,0:T(8,128)(2,1)S(1)}, bf16[64,3840]{1,0:T(8,128)(2,1)S(1)}, u32[]{:S(2)}, u32[]{:S(2)}) collective-permute-start(bf16[64,3840]{1,0:T(8,128)(2,1)S(1)} %collective-permute-done.packed), channel_id=1, source_target_pairs={{0,8},{1,9},{2,10},{3,11},{4,12},{5,13},{6,14},{7,15},{8,16},{9,17... | collective-permute-start | bytes 1474568 | tf_op jit(solution)/shard_map/ppermute | solution.py:30
  43.9 1.7 %copy-start = (bf16[3072,384]{1,0:T(8,128)(2,1)S(1)}, bf16[3072,384]{1,0:T(8,128)(2,1)}, u32[]{:S(2)}) copy-start(bf16[3072,384]{1,0:T(8,128)(2,1)} %w_input.7) | copy-start | bytes 7077892
  45.6 1.7 %copy-start.2 = (bf16[384,3072]{1,0:T(8,128)(2,1)S(1)}, bf16[384,3072]{1,0:T(8,128)(2,1)}, u32[]{:S(2)}) copy-start(bf16[384,3072]{1,0:T(8,128)(2,1)} %w_output.7) | copy-start | bytes 7077892
  48.9 13.7 %collective-permute-start.3 = (bf16[64,3840]{1,0:T(8,128)(2,1)S(1)}, bf16[64,3840]{1,0:T(8,128)(2,1)S(1)}, u32[]{:S(2)}, u32[]{:S(2)}) collective-permute-start(bf16[64,3840]{1,0:T(8,128)(2,1)S(1)} %shard_map.58), channel_id=1, source_target_pairs={{0,8},{1,9},{2,10},{3,11},{4,12},{5,13},{6,14},{7,15},{8,16},{9,17... | collective-permute-start | bytes 1474568 | tf_op jit(solution)/shard_map/ppermute | solution.py:30
  53.4 8.0 %copy-start.1 = (bf16[3072,384]{1,0:T(8,128)(2,1)S(1)}, bf16[3072,384]{1,0:T(8,128)(2,1)}, u32[]{:S(2)}) copy-start(bf16[3072,384]{1,0:T(8,128)(2,1)} %w_input.7) | copy-start | bytes 7077892
  53.5 8.0 %copy-start.3 = (bf16[384,3072]{1,0:T(8,128)(2,1)S(1)}, bf16[384,3072]{1,0:T(8,128)(2,1)}, u32[]{:S(2)}) copy-start(bf16[384,3072]{1,0:T(8,128)(2,1)} %w_output.7) | copy-start | bytes 7077892
  53.5 14.7 %collective-permute-start.1 = (bf16[64,3840]{1,0:T(8,128)(2,1)S(1)}, bf16[64,3840]{1,0:T(8,128)(2,1)S(1)}, u32[]{:S(2)}, u32[]{:S(2)}) collective-permute-start(bf16[64,3840]{1,0:T(8,128)(2,1)S(1)} %shard_map.57), channel_id=1, source_target_pairs={{0,88},{1,89},{2,90},{3,91},{4,92},{5,93},{6,94},{7,95},{8,0},{9,1... | collective-permute-start | bytes 1474568 | tf_op jit(solution)/shard_map/ppermute | solution.py:30
  57.9 22.2 %collective-permute-start.5 = (bf16[64,3840]{1,0:T(8,128)(2,1)S(1)}, bf16[64,3840]{1,0:T(8,128)(2,1)S(1)}, u32[]{:S(2)}, u32[]{:S(2)}) collective-permute-start(bf16[64,3840]{1,0:T(8,128)(2,1)S(1)} %shard_map.59), channel_id=1, source_target_pairs={{0,80},{1,81},{2,82},{3,83},{4,84},{5,85},{6,86},{7,87},{8,88},{9,... | collective-permute-start | bytes 1474568 | tf_op jit(solution)/shard_map/ppermute | solution.py:30
  62.6 37.9 %copy-start.5 = (f32[3072]{0:T(1024)S(1)}, f32[3072]{0:T(1024)}, u32[]{:S(2)}) copy-start(f32[3072]{0:T(1024)} %param.9) | copy-start | bytes 36868

commit v3 on v2

--- a/solution.py
+++ b/solution.py
@@ -68,11 +68,11 @@
     left = packed[:, features:]
     for q in range(QUARTERS):
         block[MAIN:, q * part : (q + 1) * part] = dot(picks(q), left).astype(jnp.bfloat16)
-    pre = dot(block[...], w_input[...]) + b_input[...]
+    pre = dot(block[...], w_input[...]) + b_input[...].reshape(1, -1)
     return (0.5 * pre * (1.0 + lax.erf(pre * (0.5**0.5)))).astype(jnp.bfloat16)
 
 
-def away_kernel(packed, w_input, b_input, w_output, out, block):
+def away_kernel(packed, w_input, b_input, w_output, earlier, out, block):
     hidden = hidden_of(packed, w_input, b_input, block)
     features = w_output.shape[1]
     part = features // QUARTERS
@@ -117,7 +117,7 @@
     features = total.shape[1]
     part = features // QUARTERS
     me = lax.axis_index("z")
-    bias = b_output[...]
+    bias = b_output[...].reshape(1, -1)
     summed = jnp.zeros((EIGHT, got.shape[1]), jnp.float32)
     others = got[...].astype(jnp.float32)
     for z in range(Z):
@@ -133,24 +133,24 @@
             out[EIGHT + r : EIGHT + r + 1, cols] = mine[:, cols] + summed[row : row + 1, features:]
 
 
-def call(kernel, outs, args, scratch=(), flops=0):
+def call(kernel, outs, args, scratch=(), flops=0, after=()):
     moved = sum(a.size * a.dtype.itemsize for a in args) + sum(o.size * o.dtype.itemsize for o in outs)
     return pl.pallas_call(
         kernel,
         out_shape=outs,
-        in_specs=[pl.BlockSpec(memory_space=pltpu.VMEM)] * len(args),
+        in_specs=[pl.BlockSpec(memory_space=pltpu.VMEM)] * len(args) + [pl.BlockSpec(memory_space=pl.ANY)] * len(after),
         out_specs=tuple(pl.BlockSpec(memory_space=pltpu.VMEM) for _ in outs),
         scratch_shapes=scratch,
         compiler_params=pltpu.CompilerParams(vmem_limit_bytes=32 << 20),
         cost_estimate=pl.CostEstimate(flops=flops, bytes_accessed=moved, transcendentals=0),
-    )(*args)
+    )(*args, *after)
 
 
 def body(tokens, w_input, b_input, w_output, b_output):
     features, units = w_input.shape
     wide = features + features // QUARTERS
     rows = MAIN + LEFT
-    weights = (w_input, b_input.reshape(1, -1), w_output)
+    weights = (w_input, b_input, w_output)
     packed = jax.ShapeDtypeStruct((MAIN, wide), jnp.bfloat16)
     sums = jax.ShapeDtypeStruct((rows, features), jnp.float32)
     block = (pltpu.VMEM((rows, features), jnp.bfloat16),)
@@ -160,18 +160,19 @@
     mine = exchange_z(copies)
     up1 = along_y(mine, 1)
     (own,) = call(own_kernel, (sums,), (mine,) + weights, block, flops)
+    up1, own = lax.optimization_barrier((up1, own))
     up2 = along_y(up1, 1)
     down1 = along_y(mine, -1)
     back = []
     for away, k in ((up1, -1), (down1, 1), (up2, -2)):
-        (part,) = call(away_kernel, (packed,), (away,) + weights, block, flops)
+        (part,) = call(away_kernel, (packed,), (away,) + weights, block, flops, (own,))
         back.append(along_y(part, k))
     total, outgoing = call(add_kernel, (sums, packed), (own, *back))
     got = exchange_z(outgoing)
     (out,) = call(
         last_kernel,
         (jax.ShapeDtypeStruct((EIGHT + REST, features), jnp.float32),),
-        (total, got, b_output.reshape(1, -1)),
+        (total, got, b_output),
     )
     return out
 

time: 102 us -> 98.2 us (0.963)
  the two profiles are of different devices: /device:TPU:43 before, /device:TPU:6 now
where the time goes in v3:
time: 98.2 us; the launch traced here: 97.3 us
  blocking collectives  42.8 us (44%)
  waiting for transfers between devices  22.7 us (23%)
  starting transfers between devices  18.9 us (19%)
  Pallas kernels  7.8 us (8%)
  local copies, waits for them, and re-layouts  4.92 us (5%)
    all_to_all x2, blocking collectives, exchange_z(): lax.all_to_all(blocks.reshape(Z, EIGHT, -1), 'z', 0, 0, tiled=True)  42.8 us
    ppermute x6, waiting for transfers between devices, along_y(): lax.ppermute(block, NAMES, pairs(lambda x, y, c, z: (x, y + k * (1 - 2 *...  22.7 us
    ppermute x6, starting transfers between devices, along_y(): lax.ppermute(block, NAMES, pairs(lambda x, y, c, z: (x, y + k * (1 - 2 *...  18.9 us
    pallas_call x7, Pallas kernels, call(): pl.pallas_call(kernel, out_shape=outs, in_specs=[pl.BlockSpec(memory_spac...  7.8 us
    unnamed x16, local copies, waits for them, and re-layouts  4.92 us
  transfers between devices with their start and end apart: 6, of which 4 were waited for; matrix products, arithmetic and copies ran while one was open for 0% of the time, Pallas kernels for 6%

profile of v3, /device:TPU:6, one launch (start us, length us, event | category | flops | bytes accessed | tf_op | source)
XLA Modules:
  0.0 97.3 jit_solution(8361067851105711661)
XLA Ops:
  0.0 0.9 copy-done.4
  0.9 26.9 %all_to_all.10 = bf16[8,8,3840]{2,1,0:T(8,128)(2,1)S(1)} all-to-all(bf16[8,8,3840]{2,1,0:T(8,128)(2,1)S(1)} %bitcast.8), channel_id=1, replica_groups=mesh['x'=4,'y_hi'=2,'core'=2,'y_lo'=4,'z'=8] {'z'}, dimensions={0} | all-to-all | bytes 983040 | tf_op jit(solution)/shard_map/all_to_all | solution.py:34
  27.8 3.5 %collective-permute-start = (bf16[64,3840]{1,0:T(8,128)(2,1)S(1)}, bf16[64,3840]{1,0:T(8,128)(2,1)S(1)}, u32[]{:S(2)}, u32[]{:S(2)}) collective-permute-start(bf16[64,3840]{1,0:T(8,128)(2,1)S(1)} %bitcast.4), channel_id=1, source_target_pairs={{0,8},{1,9},{2,10},{3,11},{4,12},{5,13},{6,14},{7,15},{8,16},{9,17... | collective-permute-start | bytes 1474568 | tf_op jit(solution)/shard_map/ppermute | solution.py:30
  31.3 3.8 %collective-permute-start.2 = (bf16[64,3840]{1,0:T(8,128)(2,1)S(1)}, bf16[64,3840]{1,0:T(8,128)(2,1)S(1)}, u32[]{:S(2)}, u32[]{:S(2)}) collective-permute-start(bf16[64,3840]{1,0:T(8,128)(2,1)S(1)} %bitcast.5), channel_id=1, source_target_pairs={{0,88},{1,89},{2,90},{3,91},{4,92},{5,93},{6,94},{7,95},{8,0},{9,1... | collective-permute-start | bytes 1474568 | tf_op jit(solution)/shard_map/ppermute | solution.py:30
  35.1 0.0 copy-start
  35.2 1.7 %copy-done = bf16[3072,384]{1,0:T(8,128)(2,1)S(1)} copy-done((bf16[3072,384]{1,0:T(8,128)(2,1)S(1)}, bf16[3072,384]{1,0:T(8,128)(2,1)}, u32[]{:S(2)}) %copy-start) | copy-done | bytes 2359320
  36.8 1.7 %copy-done.2 = bf16[384,3072]{1,0:T(8,128)(2,1)S(1)} copy-done((bf16[384,3072]{1,0:T(8,128)(2,1)S(1)}, bf16[384,3072]{1,0:T(8,128)(2,1)}, u32[]{:S(2)}) %copy-start.2) | copy-done | bytes 2359320
  38.5 0.7 copy-done.5
  39.2 1.2 %shard_map.56.earlier.own = f32[80,3072]{1,0:T(8,128)S(1)} custom-call(bf16[64,3840]{1,0:T(8,128)(2,1)S(1)} %bitcast.6, bf16[3072,384]{1,0:T(8,128)(2,1)S(1)} %copy-done, f32[384]{0:T(512)S(1)} %copy-done.5, bf16[384,3072]{1,0:T(8,128)(2,1)S(1)} %copy-done.2), custom_call_target="tpu_custom_call" | custom-call | flops 377487360 | bytes 6194688 | tf_op jit(solution)/shard_map/pallas_call | solution.py:138
  40.3 0.0 copy-start.6
  40.4 2.8 %collective-permute-done.packed = bf16[64,3840]{1,0:T(8,128)(2,1)S(1)} collective-permute-done((bf16[64,3840]{1,0:T(8,128)(2,1)S(1)}, bf16[64,3840]{1,0:T(8,128)(2,1)S(1)}, u32[]{:S(2)}, u32[]{:S(2)}) %collective-permute-start) | collective-permute-done | bytes 491552 | tf_op jit(solution)/shard_map/ppermute | solution.py:30
  43.2 3.1 %collective-permute-start.4 = (bf16[64,3840]{1,0:T(8,128)(2,1)S(1)}, bf16[64,3840]{1,0:T(8,128)(2,1)S(1)}, u32[]{:S(2)}, u32[]{:S(2)}) collective-permute-start(bf16[64,3840]{1,0:T(8,128)(2,1)S(1)} %collective-permute-done.packed), channel_id=1, source_target_pairs={{0,8},{1,9},{2,10},{3,11},{4,12},{5,13},{6,14},{7,15},{8,16},{9,17... | collective-permute-start | bytes 1474568 | tf_op jit(solution)/shard_map/ppermute | solution.py:30
  46.3 1.7 %shard_map.57 = bf16[64,3840]{1,0:T(8,128)(2,1)S(1)} custom-call(bf16[64,3840]{1,0:T(8,128)(2,1)S(1)} %collective-permute-done.packed, bf16[3072,384]{1,0:T(8,128)(2,1)S(1)} %copy-done.1, f32[384]{0:T(512)S(1)} %copy-done.5, bf16[384,3072]{1,0:T(8,128)(2,1)S(1)} %copy-done.3, f32[80,3072]{1,0:T(8,128)S(1)} %shard_map.56.earlier.own), custom_call_target="tpu_custom_call" | custom-call | flops 377487360 | bytes 5703168 | tf_op jit(solution)/shard_map/pallas_call | solution.py:138
  48.0 4.6 %collective-permute-start.1 = (bf16[64,3840]{1,0:T(8,128)(2,1)S(1)}, bf16[64,3840]{1,0:T(8,128)(2,1)S(1)}, u32[]{:S(2)}, u32[]{:S(2)}) collective-permute-start(bf16[64,3840]{1,0:T(8,128)(2,1)S(1)} %shard_map.57), channel_id=1, source_target_pairs={{0,88},{1,89},{2,90},{3,91},{4,92},{5,93},{6,94},{7,95},{8,0},{9,1... | collective-permute-start | bytes 1474568 | tf_op jit(solution)/shard_map/ppermute | solution.py:30
  52.7 1.6 %shard_map.58 = bf16[64,3840]{1,0:T(8,128)(2,1)S(1)} custom-call(bf16[64,3840]{1,0:T(8,128)(2,1)S(1)} %collective-permute-done.2.packed, bf16[3072,384]{1,0:T(8,128)(2,1)S(1)} %copy-done.1, f32[384]{0:T(512)S(1)} %copy-done.6, bf16[384,3072]{1,0:T(8,128)(2,1)S(1)} %copy-done.3, f32[80,3072]{1,0:T(8,128)S(1)} %shard_map.56.earlier.own), custom_call_target="tpu_custom_call" | custom-call | flops 377487360 | bytes 5703168 | tf_op jit(solution)/shard_map/pallas_call | solution.py:138
  54.3 1.9 %collective-permute-start.3 = (bf16[64,3840]{1,0:T(8,128)(2,1)S(1)}, bf16[64,3840]{1,0:T(8,128)(2,1)S(1)}, u32[]{:S(2)}, u32[]{:S(2)}) collective-permute-start(bf16[64,3840]{1,0:T(8,128)(2,1)S(1)} %shard_map.58), channel_id=1, source_target_pairs={{0,8},{1,9},{2,10},{3,11},{4,12},{5,13},{6,14},{7,15},{8,16},{9,17... | collective-permute-start | bytes 1474568 | tf_op jit(solution)/shard_map/ppermute | solution.py:30
  56.2 4.9 %collective-permute-done.4.packed = bf16[64,3840]{1,0:T(8,128)(2,1)S(1)} collective-permute-done((bf16[64,3840]{1,0:T(8,128)(2,1)S(1)}, bf16[64,3840]{1,0:T(8,128)(2,1)S(1)}, u32[]{:S(2)}, u32[]{:S(2)}) %collective-permute-start.4) | collective-permute-done | bytes 491552 | tf_op jit(solution)/shard_map/ppermute | solution.py:30
  61.1 1.7 %shard_map.59 = bf16[64,3840]{1,0:T(8,128)(2,1)S(1)} custom-call(bf16[64,3840]{1,0:T(8,128)(2,1)S(1)} %collective-permute-done.4.packed, bf16[3072,384]{1,0:T(8,128)(2,1)S(1)} %copy-done.1, f32[384]{0:T(512)S(1)} %copy-done.6, bf16[384,3072]{1,0:T(8,128)(2,1)S(1)} %copy-done.3, f32[80,3072]{1,0:T(8,128)S(1)} %shard_map.56.earlier.own), custom_call_target="tpu_custom_call" | custom-call | flops 377487360 | bytes 5703168 | tf_op jit(solution)/shard_map/pallas_call | solution.py:138
  62.8 1.9 %collective-permute-start.5 = (bf16[64,3840]{1,0:T(8,128)(2,1)S(1)}, bf16[64,3840]{1,0:T(8,128)(2,1)S(1)}, u32[]{:S(2)}, u32[]{:S(2)}) collective-permute-start(bf16[64,3840]{1,0:T(8,128)(2,1)S(1)} %shard_map.59), channel_id=1, source_target_pairs={{0,80},{1,81},{2,82},{3,83},{4,84},{5,85},{6,86},{7,87},{8,88},{9,... | collective-permute-start | bytes 1474568 | tf_op jit(solution)/shard_map/ppermute | solution.py:30
  64.7 11.9 %collective-permute-done.3.two = bf16[64,3840]{1,0:T(8,128)(2,1)S(1)} collective-permute-done((bf16[64,3840]{1,0:T(8,128)(2,1)S(1)}, bf16[64,3840]{1,0:T(8,128)(2,1)S(1)}, u32[]{:S(2)}, u32[]{:S(2)}) %collective-permute-start.3) | collective-permute-done | bytes 491552 | tf_op jit(solution)/shard_map/ppermute | solution.py:30
  76.6 3.0 %collective-permute-done.5.three = bf16[64,3840]{1,0:T(8,128)(2,1)S(1)} collective-permute-done((bf16[64,3840]{1,0:T(8,128)(2,1)S(1)}, bf16[64,3840]{1,0:T(8,128)(2,1)S(1)}, u32[]{:S(2)}, u32[]{:S(2)}) %collective-permute-start.5) | collective-permute-done | bytes 491552 | tf_op jit(solution)/shard_map/ppermute | solution.py:30
  79.7 0.8 shard_map.60
  80.5 15.9 %all_to_all.11 = bf16[8,8,3840]{2,1,0:T(8,128)(2,1)S(1)} all-to-all(bf16[8,8,3840]{2,1,0:T(8,128)(2,1)S(1)} %bitcast.9), channel_id=1, replica_groups=mesh['x'=4,'y_hi'=2,'core'=2,'y_lo'=4,'z'=8] {'z'}, dimensions={0} | all-to-all | bytes 983040 | tf_op jit(solution)/shard_map/all_to_all | solution.py:34
  96.4 0.9 shard_map.61
  (13 shorter events, 0.1 us)
Async XLA Ops:
  0.0 0.9 copy-start.4
  27.8 15.3 %collective-permute-start = (bf16[64,3840]{1,0:T(8,128)(2,1)S(1)}, bf16[64,3840]{1,0:T(8,128)(2,1)S(1)}, u32[]{:S(2)}, u32[]{:S(2)}) collective-permute-start(bf16[64,3840]{1,0:T(8,128)(2,1)S(1)} %bitcast.4), channel_id=1, source_target_pairs={{0,8},{1,9},{2,10},{3,11},{4,12},{5,13},{6,14},{7,15},{8,16},{9,17... | collective-permute-start | bytes 1474568 | tf_op jit(solution)/shard_map/ppermute | solution.py:30
  31.3 21.3 %collective-permute-start.2 = (bf16[64,3840]{1,0:T(8,128)(2,1)S(1)}, bf16[64,3840]{1,0:T(8,128)(2,1)S(1)}, u32[]{:S(2)}, u32[]{:S(2)}) collective-permute-start(bf16[64,3840]{1,0:T(8,128)(2,1)S(1)} %bitcast.5), channel_id=1, source_target_pairs={{0,88},{1,89},{2,90},{3,91},{4,92},{5,93},{6,94},{7,95},{8,0},{9,1... | collective-permute-start | bytes 1474568 | tf_op jit(solution)/shard_map/ppermute | solution.py:30
  35.1 1.7 %copy-start = (bf16[3072,384]{1,0:T(8,128)(2,1)S(1)}, bf16[3072,384]{1,0:T(8,128)(2,1)}, u32[]{:S(2)}) copy-start(bf16[3072,384]{1,0:T(8,128)(2,1)} %w_input.7) | copy-start | bytes 7077892
  36.8 1.7 %copy-start.2 = (bf16[384,3072]{1,0:T(8,128)(2,1)S(1)}, bf16[384,3072]{1,0:T(8,128)(2,1)}, u32[]{:S(2)}) copy-start(bf16[384,3072]{1,0:T(8,128)(2,1)} %w_output.7) | copy-start | bytes 7077892
  38.5 0.7 copy-start.5
  39.2 7.2 %copy-start.1 = (bf16[3072,384]{1,0:T(8,128)(2,1)S(1)}, bf16[3072,384]{1,0:T(8,128)(2,1)}, u32[]{:S(2)}) copy-start(bf16[3072,384]{1,0:T(8,128)(2,1)} %w_input.7) | copy-start | bytes 7077892
  39.2 7.2 %copy-start.3 = (bf16[384,3072]{1,0:T(8,128)(2,1)S(1)}, bf16[384,3072]{1,0:T(8,128)(2,1)}, u32[]{:S(2)}) copy-start(bf16[384,3072]{1,0:T(8,128)(2,1)} %w_output.7) | copy-start | bytes 7077892
  40.3 12.3 %copy-start.6 = (f32[384]{0:T(512)S(1)}, f32[384]{0:T(512)}, u32[]{:S(2)}) copy-start(f32[384]{0:T(512)} %b_input.7) | copy-start | bytes 4612
  43.2 17.9 %collective-permute-start.4 = (bf16[64,3840]{1,0:T(8,128)(2,1)S(1)}, bf16[64,3840]{1,0:T(8,128)(2,1)S(1)}, u32[]{:S(2)}, u32[]{:S(2)}) collective-permute-start(bf16[64,3840]{1,0:T(8,128)(2,1)S(1)} %collective-permute-done.packed), channel_id=1, source_target_pairs={{0,8},{1,9},{2,10},{3,11},{4,12},{5,13},{6,14},{7,15},{8,16},{9,17... | collective-permute-start | bytes 1474568 | tf_op jit(solution)/shard_map/ppermute | solution.py:30
  48.0 16.7 %collective-permute-start.1 = (bf16[64,3840]{1,0:T(8,128)(2,1)S(1)}, bf16[64,3840]{1,0:T(8,128)(2,1)S(1)}, u32[]{:S(2)}, u32[]{:S(2)}) collective-permute-start(bf16[64,3840]{1,0:T(8,128)(2,1)S(1)} %shard_map.57), channel_id=1, source_target_pairs={{0,88},{1,89},{2,90},{3,91},{4,92},{5,93},{6,94},{7,95},{8,0},{9,1... | collective-permute-start | bytes 1474568 | tf_op jit(solution)/shard_map/ppermute | solution.py:30
  54.3 22.3 %collective-permute-start.3 = (bf16[64,3840]{1,0:T(8,128)(2,1)S(1)}, bf16[64,3840]{1,0:T(8,128)(2,1)S(1)}, u32[]{:S(2)}, u32[]{:S(2)}) collective-permute-start(bf16[64,3840]{1,0:T(8,128)(2,1)S(1)} %shard_map.58), channel_id=1, source_target_pairs={{0,8},{1,9},{2,10},{3,11},{4,12},{5,13},{6,14},{7,15},{8,16},{9,17... | collective-permute-start | bytes 1474568 | tf_op jit(solution)/shard_map/ppermute | solution.py:30
  62.8 33.6 %copy-start.7 = (f32[3072]{0:T(1024)S(1)}, f32[3072]{0:T(1024)}, u32[]{:S(2)}) copy-start(f32[3072]{0:T(1024)} %b_output.1) | copy-start | bytes 36868
  62.8 16.9 %collective-permute-start.5 = (bf16[64,3840]{1,0:T(8,128)(2,1)S(1)}, bf16[64,3840]{1,0:T(8,128)(2,1)S(1)}, u32[]{:S(2)}, u32[]{:S(2)}) collective-permute-start(bf16[64,3840]{1,0:T(8,128)(2,1)S(1)} %shard_map.59), channel_id=1, source_target_pairs={{0,80},{1,81},{2,82},{3,83},{4,84},{5,85},{6,86},{7,87},{8,88},{9,... | collective-permute-start | bytes 1474568 | tf_op jit(solution)/shard_map/ppermute | solution.py:30

commit v4 on v3

--- a/solution.py
+++ b/solution.py
@@ -61,15 +61,22 @@
     out[:, features:] = jnp.concatenate(rest * Z, 0).astype(jnp.bfloat16)
 
 
-def hidden_of(packed, w_input, b_input, block):
-    features = w_input.shape[0]
+def expand(packed, block):
+    features = block.shape[1]
     part = features // QUARTERS
     block[:MAIN] = packed[:, :features]
     left = packed[:, features:]
     for q in range(QUARTERS):
         block[MAIN:, q * part : (q + 1) * part] = dot(picks(q), left).astype(jnp.bfloat16)
-    pre = dot(block[...], w_input[...]) + b_input[...].reshape(1, -1)
+
+
+def gelu(pre):
     return (0.5 * pre * (1.0 + lax.erf(pre * (0.5**0.5)))).astype(jnp.bfloat16)
+
+
+def hidden_of(packed, w_input, b_input, block):
+    expand(packed, block)
+    return gelu(dot(block[...], w_input[...]) + b_input[...].reshape(1, -1))
 
 
 def away_kernel(packed, w_input, b_input, w_output, earlier, out, block):
@@ -85,12 +92,32 @@
     out[:, features:] = left.astype(jnp.bfloat16)
 
 
-def own_kernel(packed, w_input, b_input, w_output, out, block):
-    hidden = hidden_of(packed, w_input, b_input, block)
-    part = w_output.shape[1] // QUARTERS
-    for q in range(QUARTERS):
-        at = slice(q * part, (q + 1) * part)
-        out[:, at] = dot(hidden, w_output[:, at])
+def own_kernel(packed, w_input, b_input, w_output, out, w_input_near, b_input_near, w_output_near, block, arrived):
+    features = w_input.shape[0]
+    part = features // QUARTERS
+    quarters = [slice(q * part, (q + 1) * part) for q in range(QUARTERS)]
+    moves = [pltpu.make_async_copy(b_input, b_input_near, arrived.at[2 * QUARTERS])]
+    moves += [pltpu.make_async_copy(w_input.at[at], w_input_near.at[at], arrived.at[q]) for q, at in enumerate(quarters)]
+    deep = w_output.shape[0] // QUARTERS
+    moves += [
+        pltpu.make_async_copy(
+            w_output.at[pl.ds(q * deep, deep)], w_output_near.at[pl.ds(q * deep, deep)], arrived.at[QUARTERS + q]
+        )
+        for q in range(QUARTERS)
+    ]
+    for move in moves:
+        move.start()
+    expand(packed, block)
+    moves[0].wait()
+    pre = b_input_near[...].reshape(1, -1)
+    for q, at in enumerate(quarters):
+        moves[1 + q].wait()
+        pre = pre + dot(block[:, at], w_input_near[at])
+    hidden = gelu(pre)
+    for move in moves[1 + QUARTERS :]:
+        move.wait()
+    for at in quarters:
+        out[:, at] = dot(hidden, w_output_near[:, at])
 
 
 def add_kernel(own, one, two, three, total, packed):
@@ -133,12 +160,12 @@
             out[EIGHT + r : EIGHT + r + 1, cols] = mine[:, cols] + summed[row : row + 1, features:]
 
 
-def call(kernel, outs, args, scratch=(), flops=0, after=()):
-    moved = sum(a.size * a.dtype.itemsize for a in args) + sum(o.size * o.dtype.itemsize for o in outs)
+def call(kernel, outs, args, scratch=(), flops=0, after=(), in_hbm=()):
+    moved = sum(a.size * a.dtype.itemsize for a in args)
     return pl.pallas_call(
         kernel,
         out_shape=outs,
-        in_specs=[pl.BlockSpec(memory_space=pltpu.VMEM)] * len(args) + [pl.BlockSpec(memory_space=pl.ANY)] * len(after),
+        in_specs=[pl.BlockSpec(memory_space=pltpu.HBM if i in in_hbm else pltpu.VMEM) for i in range(len(args))] + [pl.BlockSpec(memory_space=pl.ANY)] * len(after),
         out_specs=tuple(pl.BlockSpec(memory_space=pltpu.VMEM) for _ in outs),
         scratch_shapes=scratch,
         compiler_params=pltpu.CompilerParams(vmem_limit_bytes=32 << 20),
@@ -151,6 +178,7 @@
     wide = features + features // QUARTERS
     rows = MAIN + LEFT
     weights = (w_input, b_input, w_output)
+    inside = tuple(pltpu.VMEM(w.shape, w.dtype) for w in weights)
     packed = jax.ShapeDtypeStruct((MAIN, wide), jnp.bfloat16)
     sums = jax.ShapeDtypeStruct((rows, features), jnp.float32)
     block = (pltpu.VMEM((rows, features), jnp.bfloat16),)
@@ -159,7 +187,15 @@
     (copies,) = call(copies_kernel, (packed,), (tokens,))
     mine = exchange_z(copies)
     up1 = along_y(mine, 1)
-    (own,) = call(own_kernel, (sums,), (mine,) + weights, block, flops)
+    own, *weights = call(
+        own_kernel,
+        (sums,) + inside,
+        (mine,) + tuple(pltpu.with_memory_space_constraint(w, pltpu.HBM) for w in weights),
+        block + (pltpu.SemaphoreType.DMA((2 * QUARTERS + 1,)),),
+        flops,
+        in_hbm=(1, 2, 3),
+    )
+    weights = tuple(pltpu.with_memory_space_constraint(w, pltpu.VMEM) for w in weights)
     up1, own = lax.optimization_barrier((up1, own))
     up2 = along_y(up1, 1)
     down1 = along_y(mine, -1)

time: 98.2 us -> 97.4 us (level)
  local copies, waits for them, and re-layouts: 4.92 us -> 0.9 us
  Pallas kernels: 7.8 us -> 9.61 us
  blocking collectives: 42.8 us -> 44 us
    unnamed x16 -> x4, local copies, waits for them, and re-layouts: 4.92 us -> 0.9 us
    pallas_call x7, Pallas kernels: 7.8 us -> 9.61 us  [call(): pl.pallas_call(kernel, out_shape=outs, in_specs=[pl.BlockSpec(memory_spac...]
    all_to_all x2, blocking collectives: 42.8 us -> 44 us  [exchange_z(): lax.all_to_all(blocks.reshape(Z, EIGHT, -1), 'z', 0, 0, tiled=True)]
  transfers between devices with their start and end apart: 6 -> 6, of which waited for: 4 -> 4; matrix products, arithmetic and copies ran while one was open for 0% -> 0% of each run, Pallas kernels for 6% -> 8%
where the time goes in v4:
time: 97.4 us; the launch traced here: 97 us
  blocking collectives  44 us (45%)
  waiting for transfers between devices  23.4 us (24%)
  starting transfers between devices  18.9 us (19%)
  Pallas kernels  9.61 us (10%)
    all_to_all x2, blocking collectives, exchange_z(): lax.all_to_all(blocks.reshape(Z, EIGHT, -1), 'z', 0, 0, tiled=True)  44 us
    ppermute x6, waiting for transfers between devices, along_y(): lax.ppermute(block, NAMES, pairs(lambda x, y, c, z: (x, y + k * (1 - 2 *...  23.4 us
    ppermute x6, starting transfers between devices, along_y(): lax.ppermute(block, NAMES, pairs(lambda x, y, c, z: (x, y + k * (1 - 2 *...  18.9 us
    pallas_call x7, Pallas kernels, call(): pl.pallas_call(kernel, out_shape=outs, in_specs=[pl.BlockSpec(memory_spac...  9.61 us
  transfers between devices with their start and end apart: 6, of which 4 were waited for; matrix products, arithmetic and copies ran while one was open for 0% of the time, Pallas kernels for 8%

profile of v4, /device:TPU:6, one launch (start us, length us, event | category | flops | bytes accessed | tf_op | source)
XLA Modules:
  0.0 97.0 jit_solution(5923452203090237786)
XLA Ops:
  0.0 0.0 copy-start
  0.0 0.9 copy-done
  0.9 26.9 %all_to_all.10 = bf16[8,8,3840]{2,1,0:T(8,128)(2,1)S(1)} all-to-all(bf16[8,8,3840]{2,1,0:T(8,128)(2,1)S(1)} %bitcast.8), channel_id=1, replica_groups=mesh['x'=4,'y_hi'=2,'core'=2,'y_lo'=4,'z'=8] {'z'}, dimensions={0} | all-to-all | bytes 983040 | tf_op jit(solution)/shard_map/all_to_all | solution.py:34
  27.8 3.5 %collective-permute-start = (bf16[64,3840]{1,0:T(8,128)(2,1)S(1)}, bf16[64,3840]{1,0:T(8,128)(2,1)S(1)}, u32[]{:S(2)}, u32[]{:S(2)}) collective-permute-start(bf16[64,3840]{1,0:T(8,128)(2,1)S(1)} %bitcast.4), channel_id=1, source_target_pairs={{0,8},{1,9},{2,10},{3,11},{4,12},{5,13},{6,14},{7,15},{8,16},{9,17... | collective-permute-start | bytes 1474568 | tf_op jit(solution)/shard_map/ppermute | solution.py:30
  31.3 3.8 %collective-permute-start.2 = (bf16[64,3840]{1,0:T(8,128)(2,1)S(1)}, bf16[64,3840]{1,0:T(8,128)(2,1)S(1)}, u32[]{:S(2)}, u32[]{:S(2)}) collective-permute-start(bf16[64,3840]{1,0:T(8,128)(2,1)S(1)} %bitcast.5), channel_id=1, source_target_pairs={{0,88},{1,89},{2,90},{3,91},{4,92},{5,93},{6,94},{7,95},{8,0},{9,1... | collective-permute-start | bytes 1474568 | tf_op jit(solution)/shard_map/ppermute | solution.py:30
  35.1 3.0 %shard_map.56 = (f32[80,3072]{1,0:T(8,128)S(1)}, bf16[3072,384]{1,0:T(8,128)(2,1)S(1)}, f32[384]{0:T(512)S(1)}, bf16[384,3072]{1,0:T(8,128)(2,1)S(1)}) custom-call(bf16[64,3840]{1,0:T(8,128)(2,1)S(1)} %bitcast.6, bf16[3072,384]{1,0:T(8,128)(2,1)} %w_input.1, f32[384]{0:T(512)} %b_input.1, bf16[384,3072]{1,0:T(8,128)(2,1)} %w_output.1), custom_call_target="tpu_custom_call" | custom-call | flops 377487360 | bytes 5211648 | tf_op jit(solution)/shard_map/pallas_call | solution.py:165
  38.1 5.0 %collective-permute-done.packed = bf16[64,3840]{1,0:T(8,128)(2,1)S(1)} collective-permute-done((bf16[64,3840]{1,0:T(8,128)(2,1)S(1)}, bf16[64,3840]{1,0:T(8,128)(2,1)S(1)}, u32[]{:S(2)}, u32[]{:S(2)}) %collective-permute-start) | collective-permute-done | bytes 491552 | tf_op jit(solution)/shard_map/ppermute | solution.py:30
  43.2 3.1 %collective-permute-start.4 = (bf16[64,3840]{1,0:T(8,128)(2,1)S(1)}, bf16[64,3840]{1,0:T(8,128)(2,1)S(1)}, u32[]{:S(2)}, u32[]{:S(2)}) collective-permute-start(bf16[64,3840]{1,0:T(8,128)(2,1)S(1)} %collective-permute-done.packed), channel_id=1, source_target_pairs={{0,8},{1,9},{2,10},{3,11},{4,12},{5,13},{6,14},{7,15},{8,16},{9,17... | collective-permute-start | bytes 1474568 | tf_op jit(solution)/shard_map/ppermute | solution.py:30
  46.3 1.7 %shard_map.57 = bf16[64,3840]{1,0:T(8,128)(2,1)S(1)} custom-call(bf16[64,3840]{1,0:T(8,128)(2,1)S(1)} %collective-permute-done.packed, bf16[3072,384]{1,0:T(8,128)(2,1)S(1)} %get-tuple-element.16.w_input, f32[384]{0:T(512)S(1)} %get-tuple-element.17.b_input, bf16[384,3072]{1,0:T(8,128)(2,1)S(1)} %get-tuple-element.18.w_output, ...), custom_call_target="tpu_custom_call" | custom-call | flops 377487360 | bytes 5211648 | tf_op jit(solution)/shard_map/pallas_call | solution.py:165
  48.0 4.6 %collective-permute-start.1 = (bf16[64,3840]{1,0:T(8,128)(2,1)S(1)}, bf16[64,3840]{1,0:T(8,128)(2,1)S(1)}, u32[]{:S(2)}, u32[]{:S(2)}) collective-permute-start(bf16[64,3840]{1,0:T(8,128)(2,1)S(1)} %shard_map.57), channel_id=1, source_target_pairs={{0,88},{1,89},{2,90},{3,91},{4,92},{5,93},{6,94},{7,95},{8,0},{9,1... | collective-permute-start | bytes 1474568 | tf_op jit(solution)/shard_map/ppermute | solution.py:30
  52.6 0.0 collective-permute-done.2.packed
  52.6 1.7 %shard_map.58 = bf16[64,3840]{1,0:T(8,128)(2,1)S(1)} custom-call(bf16[64,3840]{1,0:T(8,128)(2,1)S(1)} %collective-permute-done.2.packed, bf16[3072,384]{1,0:T(8,128)(2,1)S(1)} %get-tuple-element.16.w_input, f32[384]{0:T(512)S(1)} %get-tuple-element.17.b_input, bf16[384,3072]{1,0:T(8,128)(2,1)S(1)} %get-tuple-element.18.w_output, ...), custom_call_target="tpu_custom_call" | custom-call | flops 377487360 | bytes 5211648 | tf_op jit(solution)/shard_map/pallas_call | solution.py:165
  54.3 1.9 %collective-permute-start.3 = (bf16[64,3840]{1,0:T(8,128)(2,1)S(1)}, bf16[64,3840]{1,0:T(8,128)(2,1)S(1)}, u32[]{:S(2)}, u32[]{:S(2)}) collective-permute-start(bf16[64,3840]{1,0:T(8,128)(2,1)S(1)} %shard_map.58), channel_id=1, source_target_pairs={{0,8},{1,9},{2,10},{3,11},{4,12},{5,13},{6,14},{7,15},{8,16},{9,17... | collective-permute-start | bytes 1474568 | tf_op jit(solution)/shard_map/ppermute | solution.py:30
  56.2 5.3 %collective-permute-done.4.packed = bf16[64,3840]{1,0:T(8,128)(2,1)S(1)} collective-permute-done((bf16[64,3840]{1,0:T(8,128)(2,1)S(1)}, bf16[64,3840]{1,0:T(8,128)(2,1)S(1)}, u32[]{:S(2)}, u32[]{:S(2)}) %collective-permute-start.4) | collective-permute-done | bytes 491552 | tf_op jit(solution)/shard_map/ppermute | solution.py:30
  61.6 1.6 %shard_map.59 = bf16[64,3840]{1,0:T(8,128)(2,1)S(1)} custom-call(bf16[64,3840]{1,0:T(8,128)(2,1)S(1)} %collective-permute-done.4.packed, bf16[3072,384]{1,0:T(8,128)(2,1)S(1)} %get-tuple-element.16.w_input, f32[384]{0:T(512)S(1)} %get-tuple-element.17.b_input, bf16[384,3072]{1,0:T(8,128)(2,1)S(1)} %get-tuple-element.18.w_output, ...), custom_call_target="tpu_custom_call" | custom-call | flops 377487360 | bytes 5211648 | tf_op jit(solution)/shard_map/pallas_call | solution.py:165
  63.2 0.0 copy-start.1
  63.2 1.9 %collective-permute-start.5 = (bf16[64,3840]{1,0:T(8,128)(2,1)S(1)}, bf16[64,3840]{1,0:T(8,128)(2,1)S(1)}, u32[]{:S(2)}, u32[]{:S(2)}) collective-permute-start(bf16[64,3840]{1,0:T(8,128)(2,1)S(1)} %shard_map.59), channel_id=1, source_target_pairs={{0,80},{1,81},{2,82},{3,83},{4,84},{5,85},{6,86},{7,87},{8,88},{9,... | collective-permute-start | bytes 1474568 | tf_op jit(solution)/shard_map/ppermute | solution.py:30
  65.2 0.0 collective-permute-done.1.one
  65.2 11.1 %collective-permute-done.3.two = bf16[64,3840]{1,0:T(8,128)(2,1)S(1)} collective-permute-done((bf16[64,3840]{1,0:T(8,128)(2,1)S(1)}, bf16[64,3840]{1,0:T(8,128)(2,1)S(1)}, u32[]{:S(2)}, u32[]{:S(2)}) %collective-permute-start.3) | collective-permute-done | bytes 491552 | tf_op jit(solution)/shard_map/ppermute | solution.py:30
  76.3 1.9 %collective-permute-done.5.three = bf16[64,3840]{1,0:T(8,128)(2,1)S(1)} collective-permute-done((bf16[64,3840]{1,0:T(8,128)(2,1)S(1)}, bf16[64,3840]{1,0:T(8,128)(2,1)S(1)}, u32[]{:S(2)}, u32[]{:S(2)}) %collective-permute-start.5) | collective-permute-done | bytes 491552 | tf_op jit(solution)/shard_map/ppermute | solution.py:30
  78.2 0.8 shard_map.60
  78.9 17.1 %all_to_all.11 = bf16[8,8,3840]{2,1,0:T(8,128)(2,1)S(1)} all-to-all(bf16[8,8,3840]{2,1,0:T(8,128)(2,1)S(1)} %bitcast.9), channel_id=1, replica_groups=mesh['x'=4,'y_hi'=2,'core'=2,'y_lo'=4,'z'=8] {'z'}, dimensions={0} | all-to-all | bytes 983040 | tf_op jit(solution)/shard_map/all_to_all | solution.py:34
  96.1 0.0 copy-done.1
  96.1 0.9 shard_map.61
  (1 shorter events, 0.0 us)
Async XLA Ops:
  0.0 0.9 copy-start
  27.8 15.3 %collective-permute-start = (bf16[64,3840]{1,0:T(8,128)(2,1)S(1)}, bf16[64,3840]{1,0:T(8,128)(2,1)S(1)}, u32[]{:S(2)}, u32[]{:S(2)}) collective-permute-start(bf16[64,3840]{1,0:T(8,128)(2,1)S(1)} %bitcast.4), channel_id=1, source_target_pairs={{0,8},{1,9},{2,10},{3,11},{4,12},{5,13},{6,14},{7,15},{8,16},{9,17... | collective-permute-start | bytes 1474568 | tf_op jit(solution)/shard_map/ppermute | solution.py:30
  31.3 21.3 %collective-permute-start.2 = (bf16[64,3840]{1,0:T(8,128)(2,1)S(1)}, bf16[64,3840]{1,0:T(8,128)(2,1)S(1)}, u32[]{:S(2)}, u32[]{:S(2)}) collective-permute-start(bf16[64,3840]{1,0:T(8,128)(2,1)S(1)} %bitcast.5), channel_id=1, source_target_pairs={{0,88},{1,89},{2,90},{3,91},{4,92},{5,93},{6,94},{7,95},{8,0},{9,1... | collective-permute-start | bytes 1474568 | tf_op jit(solution)/shard_map/ppermute | solution.py:30
  43.2 18.4 %collective-permute-start.4 = (bf16[64,3840]{1,0:T(8,128)(2,1)S(1)}, bf16[64,3840]{1,0:T(8,128)(2,1)S(1)}, u32[]{:S(2)}, u32[]{:S(2)}) collective-permute-start(bf16[64,3840]{1,0:T(8,128)(2,1)S(1)} %collective-permute-done.packed), channel_id=1, source_target_pairs={{0,8},{1,9},{2,10},{3,11},{4,12},{5,13},{6,14},{7,15},{8,16},{9,17... | collective-permute-start | bytes 1474568 | tf_op jit(solution)/shard_map/ppermute | solution.py:30
  48.0 17.2 %collective-permute-start.1 = (bf16[64,3840]{1,0:T(8,128)(2,1)S(1)}, bf16[64,3840]{1,0:T(8,128)(2,1)S(1)}, u32[]{:S(2)}, u32[]{:S(2)}) collective-permute-start(bf16[64,3840]{1,0:T(8,128)(2,1)S(1)} %shard_map.57), channel_id=1, source_target_pairs={{0,88},{1,89},{2,90},{3,91},{4,92},{5,93},{6,94},{7,95},{8,0},{9,1... | collective-permute-start | bytes 1474568 | tf_op jit(solution)/shard_map/ppermute | solution.py:30
  54.3 21.9 %collective-permute-start.3 = (bf16[64,3840]{1,0:T(8,128)(2,1)S(1)}, bf16[64,3840]{1,0:T(8,128)(2,1)S(1)}, u32[]{:S(2)}, u32[]{:S(2)}) collective-permute-start(bf16[64,3840]{1,0:T(8,128)(2,1)S(1)} %shard_map.58), channel_id=1, source_target_pairs={{0,8},{1,9},{2,10},{3,11},{4,12},{5,13},{6,14},{7,15},{8,16},{9,17... | collective-permute-start | bytes 1474568 | tf_op jit(solution)/shard_map/ppermute | solution.py:30
  63.2 32.9 %copy-start.1 = (f32[3072]{0:T(1024)S(1)}, f32[3072]{0:T(1024)}, u32[]{:S(2)}) copy-start(f32[3072]{0:T(1024)} %b_output.1) | copy-start | bytes 36868
  63.2 14.9 %collective-permute-start.5 = (bf16[64,3840]{1,0:T(8,128)(2,1)S(1)}, bf16[64,3840]{1,0:T(8,128)(2,1)S(1)}, u32[]{:S(2)}, u32[]{:S(2)}) collective-permute-start(bf16[64,3840]{1,0:T(8,128)(2,1)S(1)} %shard_map.59), channel_id=1, source_target_pairs={{0,80},{1,81},{2,82},{3,83},{4,84},{5,85},{6,86},{7,87},{8,88},{9,... | collective-permute-start | bytes 1474568 | tf_op jit(solution)/shard_map/ppermute | solution.py:30

commit v5 on v3

--- a/solution.py
+++ b/solution.py
@@ -50,7 +50,10 @@
     return jnp.dot(a, b, preferred_element_type=jnp.float32)
 
 
-def copies_kernel(tokens, out):
+def copies_kernel(source, out, tokens, arrived):
+    move = pltpu.make_async_copy(source, tokens, arrived)
+    move.start()
+    move.wait()
     features = tokens.shape[1]
     part = features // QUARTERS
     rows = tokens[...].astype(jnp.float32)
@@ -61,18 +64,25 @@
     out[:, features:] = jnp.concatenate(rest * Z, 0).astype(jnp.bfloat16)
 
 
-def hidden_of(packed, w_input, b_input, block):
-    features = w_input.shape[0]
+def expand(packed, block):
+    features = block.shape[1]
     part = features // QUARTERS
     block[:MAIN] = packed[:, :features]
     left = packed[:, features:]
     for q in range(QUARTERS):
         block[MAIN:, q * part : (q + 1) * part] = dot(picks(q), left).astype(jnp.bfloat16)
-    pre = dot(block[...], w_input[...]) + b_input[...].reshape(1, -1)
+
+
+def gelu(pre):
     return (0.5 * pre * (1.0 + lax.erf(pre * (0.5**0.5)))).astype(jnp.bfloat16)
 
 
-def away_kernel(packed, w_input, b_input, w_output, earlier, out, block):
+def hidden_of(packed, w_input, b_input, block):
+    expand(packed, block)
+    return gelu(dot(block[...], w_input[...]) + b_input[...].reshape(1, -1))
+
+
+def away_kernel(packed, w_input, b_input, w_output, out, block):
     hidden = hidden_of(packed, w_input, b_input, block)
     features = w_output.shape[1]
     part = features // QUARTERS
@@ -85,6 +95,22 @@
     out[:, features:] = left.astype(jnp.bfloat16)
 
 
+def fetch_kernel(w_input, b_input, w_output, w_input_near, b_input_near, w_output_near, arrived):
+    moves = [pltpu.make_async_copy(b_input, b_input_near, arrived.at[2 * QUARTERS])]
+    for i, (far, near) in enumerate(((w_input, w_input_near), (w_output, w_output_near))):
+        deep = far.shape[0] // QUARTERS
+        moves += [
+            pltpu.make_async_copy(
+                far.at[pl.ds(q * deep, deep)], near.at[pl.ds(q * deep, deep)], arrived.at[i * QUARTERS + q]
+            )
+            for q in range(QUARTERS)
+        ]
+    for move in moves:
+        move.start()
+    for move in moves:
+        move.wait()
+
+
 def own_kernel(packed, w_input, b_input, w_output, out, block):
     hidden = hidden_of(packed, w_input, b_input, block)
     part = w_output.shape[1] // QUARTERS
@@ -93,10 +119,26 @@
         out[:, at] = dot(hidden, w_output[:, at])
 
 
-def add_kernel(own, one, two, three, total, packed):
+def near_kernel(own, one, two, total):
     features = own.shape[1]
     part = features // QUARTERS
-    terms = (one, two, three)
+    terms = (one, two)
+    main = own[:MAIN]
+    for term in terms:
+        main = main + term[:, :features].astype(jnp.float32)
+    total[:MAIN] = main
+    for q in range(QUARTERS):
+        at = slice(q * part, (q + 1) * part)
+        sums = own[MAIN:, at]
+        for term in terms:
+            sums = sums + dot(picks(q), term[:, features:])
+        total[MAIN:, at] = sums
+
+
+def add_kernel(own, far, total, packed):
+    features = own.shape[1]
+    part = features // QUARTERS
+    terms = (far,)
     main = own[:MAIN]
     for term in terms:
         main = main + term[:, :features].astype(jnp.float32)
@@ -133,12 +175,12 @@
             out[EIGHT + r : EIGHT + r + 1, cols] = mine[:, cols] + summed[row : row + 1, features:]
 
 
-def call(kernel, outs, args, scratch=(), flops=0, after=()):
-    moved = sum(a.size * a.dtype.itemsize for a in args) + sum(o.size * o.dtype.itemsize for o in outs)
+def call(kernel, outs, args, scratch=(), flops=0, after=(), in_hbm=()):
+    moved = sum(a.size * a.dtype.itemsize for a in args)
     return pl.pallas_call(
         kernel,
         out_shape=outs,
-        in_specs=[pl.BlockSpec(memory_space=pltpu.VMEM)] * len(args) + [pl.BlockSpec(memory_space=pl.ANY)] * len(after),
+        in_specs=[pl.BlockSpec(memory_space=pltpu.HBM if i in in_hbm else pltpu.VMEM) for i in range(len(args))] + [pl.BlockSpec(memory_space=pl.ANY)] * len(after),
         out_specs=tuple(pl.BlockSpec(memory_space=pltpu.VMEM) for _ in outs),
         scratch_shapes=scratch,
         compiler_params=pltpu.CompilerParams(vmem_limit_bytes=32 << 20),
@@ -151,23 +193,43 @@
     wide = features + features // QUARTERS
     rows = MAIN + LEFT
     weights = (w_input, b_input, w_output)
+    inside = tuple(pltpu.VMEM(w.shape, w.dtype) for w in weights)
     packed = jax.ShapeDtypeStruct((MAIN, wide), jnp.bfloat16)
     sums = jax.ShapeDtypeStruct((rows, features), jnp.float32)
     block = (pltpu.VMEM((rows, features), jnp.bfloat16),)
     flops = 4 * rows * features * units
 
-    (copies,) = call(copies_kernel, (packed,), (tokens,))
+    (copies,) = call(
+        copies_kernel,
+        (packed,),
+        (pltpu.with_memory_space_constraint(tokens, pltpu.HBM),),
+        (pltpu.VMEM(tokens.shape, tokens.dtype), pltpu.SemaphoreType.DMA),
+        in_hbm=(0,),
+    )
     mine = exchange_z(copies)
     up1 = along_y(mine, 1)
+    weights = call(
+        fetch_kernel,
+        inside,
+        tuple(pltpu.with_memory_space_constraint(w, pltpu.HBM) for w in weights),
+        (pltpu.SemaphoreType.DMA((2 * QUARTERS + 1,)),),
+        in_hbm=(0, 1, 2),
+    )
+    up1, *weights = lax.optimization_barrier((up1, *weights))
+    weights = tuple(pltpu.with_memory_space_constraint(w, pltpu.VMEM) for w in weights)
     (own,) = call(own_kernel, (sums,), (mine,) + weights, block, flops)
-    up1, own = lax.optimization_barrier((up1, own))
     up2 = along_y(up1, 1)
     down1 = along_y(mine, -1)
     back = []
-    for away, k in ((up1, -1), (down1, 1), (up2, -2)):
-        (part,) = call(away_kernel, (packed,), (away,) + weights, block, flops, (own,))
-        back.append(along_y(part, k))
-    total, outgoing = call(add_kernel, (sums, packed), (own, *back))
+    (part,) = call(away_kernel, (packed,), (up1,) + weights, block, flops)
+    back.append(along_y(part, -1))
+    down1, part = lax.optimization_barrier((down1, part))
+    (part,) = call(away_kernel, (packed,), (down1,) + weights, block, flops)
+    back.append(along_y(part, 1))
+    (part,) = call(away_kernel, (packed,), (up2,) + weights, block, flops)
+    back.append(along_y(part, -2))
+    (near,) = call(near_kernel, (sums,), (own, *back[:2]))
+    total, outgoing = call(add_kernel, (sums, packed), (near, back[2]))
     got = exchange_z(outgoing)
     (out,) = call(
         last_kernel,

time: 98.2 us -> 97.2 us (0.990)
  local copies, waits for them, and re-layouts: 4.92 us -> 0.01 us
  Pallas kernels: 7.8 us -> 11.3 us
  blocking collectives: 42.8 us -> 43.8 us
    unnamed x16 -> x2, local copies, waits for them, and re-layouts: 4.92 us -> 0.01 us
    pallas_call x7 -> x9, Pallas kernels: 7.8 us -> 11.3 us  [call(): pl.pallas_call(kernel, out_shape=outs, in_specs=[pl.BlockSpec(memory_spac...]
  transfers between devices with their start and end apart: 6 -> 6, of which waited for: 4 -> 4; matrix products, arithmetic and copies ran while one was open for 0% -> 0% of each run, Pallas kernels for 6% -> 9%
where the time goes in v5:
time: 97.2 us; the launch traced here: 96.9 us
  blocking collectives  43.8 us (45%)
  waiting for transfers between devices  22.8 us (23%)
  starting transfers between devices  18.9 us (19%)
  Pallas kernels  11.3 us (12%)
    all_to_all x2, blocking collectives, exchange_z(): lax.all_to_all(blocks.reshape(Z, EIGHT, -1), 'z', 0, 0, tiled=True)  43.8 us
    ppermute x6, waiting for transfers between devices, along_y(): lax.ppermute(block, NAMES, pairs(lambda x, y, c, z: (x, y + k * (1 - 2 *...  22.8 us
    ppermute x6, starting transfers between devices, along_y(): lax.ppermute(block, NAMES, pairs(lambda x, y, c, z: (x, y + k * (1 - 2 *...  18.9 us
    pallas_call x9, Pallas kernels, call(): pl.pallas_call(kernel, out_shape=outs, in_specs=[pl.BlockSpec(memory_spac...  11.3 us
  transfers between devices with their start and end apart: 6, of which 4 were waited for; matrix products, arithmetic and copies ran while one was open for 0% of the time, Pallas kernels for 9%

profile of v5, /device:TPU:6, one launch (start us, length us, event | category | flops | bytes accessed | tf_op | source)
XLA Modules:
  0.0 96.9 jit_solution(353353619024344364)
XLA Ops:
  0.0 0.9 shard_map.55
  0.9 26.9 %all_to_all.10 = bf16[8,8,3840]{2,1,0:T(8,128)(2,1)S(1)} all-to-all(bf16[8,8,3840]{2,1,0:T(8,128)(2,1)S(1)} %bitcast.8), channel_id=1, replica_groups=mesh['x'=4,'y_hi'=2,'core'=2,'y_lo'=4,'z'=8] {'z'}, dimensions={0} | all-to-all | bytes 983040 | tf_op jit(solution)/shard_map/all_to_all | solution.py:34
  27.8 3.5 %collective-permute-start = (bf16[64,3840]{1,0:T(8,128)(2,1)S(1)}, bf16[64,3840]{1,0:T(8,128)(2,1)S(1)}, u32[]{:S(2)}, u32[]{:S(2)}) collective-permute-start(bf16[64,3840]{1,0:T(8,128)(2,1)S(1)} %bitcast.4), channel_id=1, source_target_pairs={{0,8},{1,9},{2,10},{3,11},{4,12},{5,13},{6,14},{7,15},{8,16},{9,17... | collective-permute-start | bytes 1474568 | tf_op jit(solution)/shard_map/ppermute | solution.py:30
  31.3 3.8 %collective-permute-start.2 = (bf16[64,3840]{1,0:T(8,128)(2,1)S(1)}, bf16[64,3840]{1,0:T(8,128)(2,1)S(1)}, u32[]{:S(2)}, u32[]{:S(2)}) collective-permute-start(bf16[64,3840]{1,0:T(8,128)(2,1)S(1)} %bitcast.5), channel_id=1, source_target_pairs={{0,88},{1,89},{2,90},{3,91},{4,92},{5,93},{6,94},{7,95},{8,0},{9,1... | collective-permute-start | bytes 1474568 | tf_op jit(solution)/shard_map/ppermute | solution.py:30
  35.1 2.4 %shard_map.56 = (bf16[3072,384]{1,0:T(8,128)(2,1)S(1)}, f32[384]{0:T(512)S(1)}, bf16[384,3072]{1,0:T(8,128)(2,1)S(1)}) custom-call(bf16[3072,384]{1,0:T(8,128)(2,1)} %w_input.1, f32[384]{0:T(512)} %b_input.1, bf16[384,3072]{1,0:T(8,128)(2,1)} %w_output.1), custom_call_target="tpu_custom_call" | custom-call | bytes 4720128 | tf_op jit(solution)/shard_map/pallas_call | solution.py:180
  37.6 5.6 %collective-permute-done.packed = bf16[64,3840]{1,0:T(8,128)(2,1)S(1)} collective-permute-done((bf16[64,3840]{1,0:T(8,128)(2,1)S(1)}, bf16[64,3840]{1,0:T(8,128)(2,1)S(1)}, u32[]{:S(2)}, u32[]{:S(2)}) %collective-permute-start) | collective-permute-done | bytes 491552 | tf_op jit(solution)/shard_map/ppermute | solution.py:30
  43.2 3.1 %collective-permute-start.4 = (bf16[64,3840]{1,0:T(8,128)(2,1)S(1)}, bf16[64,3840]{1,0:T(8,128)(2,1)S(1)}, u32[]{:S(2)}, u32[]{:S(2)}) collective-permute-start(bf16[64,3840]{1,0:T(8,128)(2,1)S(1)} %collective-permute-done.packed), channel_id=1, source_target_pairs={{0,8},{1,9},{2,10},{3,11},{4,12},{5,13},{6,14},{7,15},{8,16},{9,17... | collective-permute-start | bytes 1474568 | tf_op jit(solution)/shard_map/ppermute | solution.py:30
  46.3 1.6 %shard_map.58 = bf16[64,3840]{1,0:T(8,128)(2,1)S(1)} custom-call(bf16[64,3840]{1,0:T(8,128)(2,1)S(1)} %collective-permute-done.packed, bf16[3072,384]{1,0:T(8,128)(2,1)S(1)} %get-tuple-element.18.w_input, f32[384]{0:T(512)S(1)} %get-tuple-element.19.b_input, bf16[384,3072]{1,0:T(8,128)(2,1)S(1)} %get-tuple-element.20.w_output), custom_call_target="tpu_custom_call" | custom-call | flops 377487360 | bytes 5211648 | tf_op jit(solution)/shard_map/pallas_call | solution.py:180
  48.0 4.6 %collective-permute-start.1 = (bf16[64,3840]{1,0:T(8,128)(2,1)S(1)}, bf16[64,3840]{1,0:T(8,128)(2,1)S(1)}, u32[]{:S(2)}, u32[]{:S(2)}) collective-permute-start(bf16[64,3840]{1,0:T(8,128)(2,1)S(1)} %shard_map.58), channel_id=1, source_target_pairs={{0,88},{1,89},{2,90},{3,91},{4,92},{5,93},{6,94},{7,95},{8,0},{9,1... | collective-permute-start | bytes 1474568 | tf_op jit(solution)/shard_map/ppermute | solution.py:30
  52.6 0.0 collective-permute-done.2.packed
  52.6 1.6 %shard_map.59 = bf16[64,3840]{1,0:T(8,128)(2,1)S(1)} custom-call(bf16[64,3840]{1,0:T(8,128)(2,1)S(1)} %collective-permute-done.2.packed, bf16[3072,384]{1,0:T(8,128)(2,1)S(1)} %get-tuple-element.18.w_input, f32[384]{0:T(512)S(1)} %get-tuple-element.19.b_input, bf16[384,3072]{1,0:T(8,128)(2,1)S(1)} %get-tuple-element.20.w_output), custom_call_target="tpu_custom_call" | custom-call | flops 377487360 | bytes 5211648 | tf_op jit(solution)/shard_map/pallas_call | solution.py:180
  54.3 1.9 %collective-permute-start.3 = (bf16[64,3840]{1,0:T(8,128)(2,1)S(1)}, bf16[64,3840]{1,0:T(8,128)(2,1)S(1)}, u32[]{:S(2)}, u32[]{:S(2)}) collective-permute-start(bf16[64,3840]{1,0:T(8,128)(2,1)S(1)} %shard_map.59), channel_id=1, source_target_pairs={{0,8},{1,9},{2,10},{3,11},{4,12},{5,13},{6,14},{7,15},{8,16},{9,17... | collective-permute-start | bytes 1474568 | tf_op jit(solution)/shard_map/ppermute | solution.py:30
  56.2 5.4 %collective-permute-done.4.packed = bf16[64,3840]{1,0:T(8,128)(2,1)S(1)} collective-permute-done((bf16[64,3840]{1,0:T(8,128)(2,1)S(1)}, bf16[64,3840]{1,0:T(8,128)(2,1)S(1)}, u32[]{:S(2)}, u32[]{:S(2)}) %collective-permute-start.4) | collective-permute-done | bytes 491552 | tf_op jit(solution)/shard_map/ppermute | solution.py:30
  61.6 1.6 %shard_map.61 = bf16[64,3840]{1,0:T(8,128)(2,1)S(1)} custom-call(bf16[64,3840]{1,0:T(8,128)(2,1)S(1)} %collective-permute-done.4.packed, bf16[3072,384]{1,0:T(8,128)(2,1)S(1)} %get-tuple-element.18.w_input, f32[384]{0:T(512)S(1)} %get-tuple-element.19.b_input, bf16[384,3072]{1,0:T(8,128)(2,1)S(1)} %get-tuple-element.20.w_output), custom_call_target="tpu_custom_call" | custom-call | flops 377487360 | bytes 5211648 | tf_op jit(solution)/shard_map/pallas_call | solution.py:180
  63.2 1.9 %collective-permute-start.5 = (bf16[64,3840]{1,0:T(8,128)(2,1)S(1)}, bf16[64,3840]{1,0:T(8,128)(2,1)S(1)}, u32[]{:S(2)}, u32[]{:S(2)}) collective-permute-start(bf16[64,3840]{1,0:T(8,128)(2,1)S(1)} %shard_map.61), channel_id=1, source_target_pairs={{0,80},{1,81},{2,82},{3,83},{4,84},{5,85},{6,86},{7,87},{8,88},{9,... | collective-permute-start | bytes 1474568 | tf_op jit(solution)/shard_map/ppermute | solution.py:30
  65.2 1.2 %shard_map.57.own = f32[80,3072]{1,0:T(8,128)S(1)} custom-call(bf16[64,3840]{1,0:T(8,128)(2,1)S(1)} %bitcast.6, bf16[3072,384]{1,0:T(8,128)(2,1)S(1)} %get-tuple-element.18.w_input, f32[384]{0:T(512)S(1)} %get-tuple-element.19.b_input, bf16[384,3072]{1,0:T(8,128)(2,1)S(1)} %get-tuple-element.20.w_output), custom_call_target="tpu_custom_call" | custom-call | flops 377487360 | bytes 5211648 | tf_op jit(solution)/shard_map/pallas_call | solution.py:180
  66.3 0.0 copy-start
  66.3 9.9 %collective-permute-done.3.two = bf16[64,3840]{1,0:T(8,128)(2,1)S(1)} collective-permute-done((bf16[64,3840]{1,0:T(8,128)(2,1)S(1)}, bf16[64,3840]{1,0:T(8,128)(2,1)S(1)}, u32[]{:S(2)}, u32[]{:S(2)}) %collective-permute-start.3) | collective-permute-done | bytes 491552 | tf_op jit(solution)/shard_map/ppermute | solution.py:30
  76.2 0.0 collective-permute-done.1.one
  76.2 0.3 shard_map.60.own
  76.5 1.9 %collective-permute-done.5.far = bf16[64,3840]{1,0:T(8,128)(2,1)S(1)} collective-permute-done((bf16[64,3840]{1,0:T(8,128)(2,1)S(1)}, bf16[64,3840]{1,0:T(8,128)(2,1)S(1)}, u32[]{:S(2)}, u32[]{:S(2)}) %collective-permute-start.5) | collective-permute-done | bytes 491552 | tf_op jit(solution)/shard_map/ppermute | solution.py:30
  78.4 0.7 shard_map.62
  79.1 16.9 %all_to_all.11 = bf16[8,8,3840]{2,1,0:T(8,128)(2,1)S(1)} all-to-all(bf16[8,8,3840]{2,1,0:T(8,128)(2,1)S(1)} %bitcast.9), channel_id=1, replica_groups=mesh['x'=4,'y_hi'=2,'core'=2,'y_lo'=4,'z'=8] {'z'}, dimensions={0} | all-to-all | bytes 983040 | tf_op jit(solution)/shard_map/all_to_all | solution.py:34
  96.0 0.9 shard_map.63
  (1 shorter events, 0.0 us)
Async XLA Ops:
  27.8 15.3 %collective-permute-start = (bf16[64,3840]{1,0:T(8,128)(2,1)S(1)}, bf16[64,3840]{1,0:T(8,128)(2,1)S(1)}, u32[]{:S(2)}, u32[]{:S(2)}) collective-permute-start(bf16[64,3840]{1,0:T(8,128)(2,1)S(1)} %bitcast.4), channel_id=1, source_target_pairs={{0,8},{1,9},{2,10},{3,11},{4,12},{5,13},{6,14},{7,15},{8,16},{9,17... | collective-permute-start | bytes 1474568 | tf_op jit(solution)/shard_map/ppermute | solution.py:30
  31.3 21.3 %collective-permute-start.2 = (bf16[64,3840]{1,0:T(8,128)(2,1)S(1)}, bf16[64,3840]{1,0:T(8,128)(2,1)S(1)}, u32[]{:S(2)}, u32[]{:S(2)}) collective-permute-start(bf16[64,3840]{1,0:T(8,128)(2,1)S(1)} %bitcast.5), channel_id=1, source_target_pairs={{0,88},{1,89},{2,90},{3,91},{4,92},{5,93},{6,94},{7,95},{8,0},{9,1... | collective-permute-start | bytes 1474568 | tf_op jit(solution)/shard_map/ppermute | solution.py:30
  43.2 18.4 %collective-permute-start.4 = (bf16[64,3840]{1,0:T(8,128)(2,1)S(1)}, bf16[64,3840]{1,0:T(8,128)(2,1)S(1)}, u32[]{:S(2)}, u32[]{:S(2)}) collective-permute-start(bf16[64,3840]{1,0:T(8,128)(2,1)S(1)} %collective-permute-done.packed), channel_id=1, source_target_pairs={{0,8},{1,9},{2,10},{3,11},{4,12},{5,13},{6,14},{7,15},{8,16},{9,17... | collective-permute-start | bytes 1474568 | tf_op jit(solution)/shard_map/ppermute | solution.py:30
  48.0 28.3 %collective-permute-start.1 = (bf16[64,3840]{1,0:T(8,128)(2,1)S(1)}, bf16[64,3840]{1,0:T(8,128)(2,1)S(1)}, u32[]{:S(2)}, u32[]{:S(2)}) collective-permute-start(bf16[64,3840]{1,0:T(8,128)(2,1)S(1)} %shard_map.58), channel_id=1, source_target_pairs={{0,88},{1,89},{2,90},{3,91},{4,92},{5,93},{6,94},{7,95},{8,0},{9,1... | collective-permute-start | bytes 1474568 | tf_op jit(solution)/shard_map/ppermute | solution.py:30
  54.3 22.0 %collective-permute-start.3 = (bf16[64,3840]{1,0:T(8,128)(2,1)S(1)}, bf16[64,3840]{1,0:T(8,128)(2,1)S(1)}, u32[]{:S(2)}, u32[]{:S(2)}) collective-permute-start(bf16[64,3840]{1,0:T(8,128)(2,1)S(1)} %shard_map.59), channel_id=1, source_target_pairs={{0,8},{1,9},{2,10},{3,11},{4,12},{5,13},{6,14},{7,15},{8,16},{9,17... | collective-permute-start | bytes 1474568 | tf_op jit(solution)/shard_map/ppermute | solution.py:30
  63.2 15.2 %collective-permute-start.5 = (bf16[64,3840]{1,0:T(8,128)(2,1)S(1)}, bf16[64,3840]{1,0:T(8,128)(2,1)S(1)}, u32[]{:S(2)}, u32[]{:S(2)}) collective-permute-start(bf16[64,3840]{1,0:T(8,128)(2,1)S(1)} %shard_map.61), channel_id=1, source_target_pairs={{0,80},{1,81},{2,82},{3,83},{4,84},{5,85},{6,86},{7,87},{8,88},{9,... | collective-permute-start | bytes 1474568 | tf_op jit(solution)/shard_map/ppermute | solution.py:30
  66.3 29.7 %copy-start = (f32[3072]{0:T(1024)S(1)}, f32[3072]{0:T(1024)}, u32[]{:S(2)}) copy-start(f32[3072]{0:T(1024)} %b_output.1) | copy-start | bytes 36868

commit v6 on v5

--- a/solution.py
+++ b/solution.py
@@ -50,10 +50,7 @@
     return jnp.dot(a, b, preferred_element_type=jnp.float32)
 
 
-def copies_kernel(source, out, tokens, arrived):
-    move = pltpu.make_async_copy(source, tokens, arrived)
-    move.start()
-    move.wait()
+def copies_kernel(tokens, out):
     features = tokens.shape[1]
     part = features // QUARTERS
     rows = tokens[...].astype(jnp.float32)
@@ -199,13 +196,7 @@
     block = (pltpu.VMEM((rows, features), jnp.bfloat16),)
     flops = 4 * rows * features * units
 
-    (copies,) = call(
-        copies_kernel,
-        (packed,),
-        (pltpu.with_memory_space_constraint(tokens, pltpu.HBM),),
-        (pltpu.VMEM(tokens.shape, tokens.dtype), pltpu.SemaphoreType.DMA),
-        in_hbm=(0,),
-    )
+    (copies,) = call(copies_kernel, (packed,), (tokens,))
     mine = exchange_z(copies)
     up1 = along_y(mine, 1)
     weights = call(

time: 97.2 us -> 97.2 us (level)
  no operation moved by 1% of the time
where the time goes in v6:
time: 97.2 us; the launch traced here: 96.9 us
  blocking collectives  43.8 us (45%)
  waiting for transfers between devices  22.8 us (23%)
  starting transfers between devices  18.9 us (19%)
  Pallas kernels  10.4 us (11%)
    all_to_all x2, blocking collectives, exchange_z(): lax.all_to_all(blocks.reshape(Z, EIGHT, -1), 'z', 0, 0, tiled=True)  43.8 us
    ppermute x6, waiting for transfers between devices, along_y(): lax.ppermute(block, NAMES, pairs(lambda x, y, c, z: (x, y + k * (1 - 2 *...  22.8 us
    ppermute x6, starting transfers between devices, along_y(): lax.ppermute(block, NAMES, pairs(lambda x, y, c, z: (x, y + k * (1 - 2 *...  18.9 us
    pallas_call x9, Pallas kernels, call(): pl.pallas_call(kernel, out_shape=outs, in_specs=[pl.BlockSpec(memory_spac...  10.4 us
  transfers between devices with their start and end apart: 6, of which 4 were waited for; matrix products, arithmetic and copies ran while one was open for 0% of the time, Pallas kernels for 9%

profile of v6, /device:TPU:6, one launch (start us, length us, event | category | flops | bytes accessed | tf_op | source)
XLA Modules:
  0.0 96.9 jit_solution(16228397792641698162)
XLA Ops:
  0.0 0.9 copy-done
  0.9 26.9 %all_to_all.10 = bf16[8,8,3840]{2,1,0:T(8,128)(2,1)S(1)} all-to-all(bf16[8,8,3840]{2,1,0:T(8,128)(2,1)S(1)} %bitcast.8), channel_id=1, replica_groups=mesh['x'=4,'y_hi'=2,'core'=2,'y_lo'=4,'z'=8] {'z'}, dimensions={0} | all-to-all | bytes 983040 | tf_op jit(solution)/shard_map/all_to_all | solution.py:34
  27.8 3.5 %collective-permute-start = (bf16[64,3840]{1,0:T(8,128)(2,1)S(1)}, bf16[64,3840]{1,0:T(8,128)(2,1)S(1)}, u32[]{:S(2)}, u32[]{:S(2)}) collective-permute-start(bf16[64,3840]{1,0:T(8,128)(2,1)S(1)} %bitcast.4), channel_id=1, source_target_pairs={{0,8},{1,9},{2,10},{3,11},{4,12},{5,13},{6,14},{7,15},{8,16},{9,17... | collective-permute-start | bytes 1474568 | tf_op jit(solution)/shard_map/ppermute | solution.py:30
  31.3 3.8 %collective-permute-start.2 = (bf16[64,3840]{1,0:T(8,128)(2,1)S(1)}, bf16[64,3840]{1,0:T(8,128)(2,1)S(1)}, u32[]{:S(2)}, u32[]{:S(2)}) collective-permute-start(bf16[64,3840]{1,0:T(8,128)(2,1)S(1)} %bitcast.5), channel_id=1, source_target_pairs={{0,88},{1,89},{2,90},{3,91},{4,92},{5,93},{6,94},{7,95},{8,0},{9,1... | collective-permute-start | bytes 1474568 | tf_op jit(solution)/shard_map/ppermute | solution.py:30
  35.1 2.4 %shard_map.56 = (bf16[3072,384]{1,0:T(8,128)(2,1)S(1)}, f32[384]{0:T(512)S(1)}, bf16[384,3072]{1,0:T(8,128)(2,1)S(1)}) custom-call(bf16[3072,384]{1,0:T(8,128)(2,1)} %w_input.1, f32[384]{0:T(512)} %b_input.1, bf16[384,3072]{1,0:T(8,128)(2,1)} %w_output.1), custom_call_target="tpu_custom_call" | custom-call | bytes 4720128 | tf_op jit(solution)/shard_map/pallas_call | solution.py:177
  37.6 5.6 %collective-permute-done.packed = bf16[64,3840]{1,0:T(8,128)(2,1)S(1)} collective-permute-done((bf16[64,3840]{1,0:T(8,128)(2,1)S(1)}, bf16[64,3840]{1,0:T(8,128)(2,1)S(1)}, u32[]{:S(2)}, u32[]{:S(2)}) %collective-permute-start) | collective-permute-done | bytes 491552 | tf_op jit(solution)/shard_map/ppermute | solution.py:30
  43.2 3.1 %collective-permute-start.4 = (bf16[64,3840]{1,0:T(8,128)(2,1)S(1)}, bf16[64,3840]{1,0:T(8,128)(2,1)S(1)}, u32[]{:S(2)}, u32[]{:S(2)}) collective-permute-start(bf16[64,3840]{1,0:T(8,128)(2,1)S(1)} %collective-permute-done.packed), channel_id=1, source_target_pairs={{0,8},{1,9},{2,10},{3,11},{4,12},{5,13},{6,14},{7,15},{8,16},{9,17... | collective-permute-start | bytes 1474568 | tf_op jit(solution)/shard_map/ppermute | solution.py:30
  46.3 1.6 %shard_map.58 = bf16[64,3840]{1,0:T(8,128)(2,1)S(1)} custom-call(bf16[64,3840]{1,0:T(8,128)(2,1)S(1)} %collective-permute-done.packed, bf16[3072,384]{1,0:T(8,128)(2,1)S(1)} %get-tuple-element.18.w_input, f32[384]{0:T(512)S(1)} %get-tuple-element.19.b_input, bf16[384,3072]{1,0:T(8,128)(2,1)S(1)} %get-tuple-element.20.w_output), custom_call_target="tpu_custom_call" | custom-call | flops 377487360 | bytes 5211648 | tf_op jit(solution)/shard_map/pallas_call | solution.py:177
  48.0 4.6 %collective-permute-start.1 = (bf16[64,3840]{1,0:T(8,128)(2,1)S(1)}, bf16[64,3840]{1,0:T(8,128)(2,1)S(1)}, u32[]{:S(2)}, u32[]{:S(2)}) collective-permute-start(bf16[64,3840]{1,0:T(8,128)(2,1)S(1)} %shard_map.58), channel_id=1, source_target_pairs={{0,88},{1,89},{2,90},{3,91},{4,92},{5,93},{6,94},{7,95},{8,0},{9,1... | collective-permute-start | bytes 1474568 | tf_op jit(solution)/shard_map/ppermute | solution.py:30
  52.6 0.0 collective-permute-done.2.packed
  52.6 1.6 %shard_map.59 = bf16[64,3840]{1,0:T(8,128)(2,1)S(1)} custom-call(bf16[64,3840]{1,0:T(8,128)(2,1)S(1)} %collective-permute-done.2.packed, bf16[3072,384]{1,0:T(8,128)(2,1)S(1)} %get-tuple-element.18.w_input, f32[384]{0:T(512)S(1)} %get-tuple-element.19.b_input, bf16[384,3072]{1,0:T(8,128)(2,1)S(1)} %get-tuple-element.20.w_output), custom_call_target="tpu_custom_call" | custom-call | flops 377487360 | bytes 5211648 | tf_op jit(solution)/shard_map/pallas_call | solution.py:177
  54.3 1.9 %collective-permute-start.3 = (bf16[64,3840]{1,0:T(8,128)(2,1)S(1)}, bf16[64,3840]{1,0:T(8,128)(2,1)S(1)}, u32[]{:S(2)}, u32[]{:S(2)}) collective-permute-start(bf16[64,3840]{1,0:T(8,128)(2,1)S(1)} %shard_map.59), channel_id=1, source_target_pairs={{0,8},{1,9},{2,10},{3,11},{4,12},{5,13},{6,14},{7,15},{8,16},{9,17... | collective-permute-start | bytes 1474568 | tf_op jit(solution)/shard_map/ppermute | solution.py:30
  56.2 5.4 %collective-permute-done.4.packed = bf16[64,3840]{1,0:T(8,128)(2,1)S(1)} collective-permute-done((bf16[64,3840]{1,0:T(8,128)(2,1)S(1)}, bf16[64,3840]{1,0:T(8,128)(2,1)S(1)}, u32[]{:S(2)}, u32[]{:S(2)}) %collective-permute-start.4) | collective-permute-done | bytes 491552 | tf_op jit(solution)/shard_map/ppermute | solution.py:30
  61.6 1.6 %shard_map.61 = bf16[64,3840]{1,0:T(8,128)(2,1)S(1)} custom-call(bf16[64,3840]{1,0:T(8,128)(2,1)S(1)} %collective-permute-done.4.packed, bf16[3072,384]{1,0:T(8,128)(2,1)S(1)} %get-tuple-element.18.w_input, f32[384]{0:T(512)S(1)} %get-tuple-element.19.b_input, bf16[384,3072]{1,0:T(8,128)(2,1)S(1)} %get-tuple-element.20.w_output), custom_call_target="tpu_custom_call" | custom-call | flops 377487360 | bytes 5211648 | tf_op jit(solution)/shard_map/pallas_call | solution.py:177
  63.2 1.9 %collective-permute-start.5 = (bf16[64,3840]{1,0:T(8,128)(2,1)S(1)}, bf16[64,3840]{1,0:T(8,128)(2,1)S(1)}, u32[]{:S(2)}, u32[]{:S(2)}) collective-permute-start(bf16[64,3840]{1,0:T(8,128)(2,1)S(1)} %shard_map.61), channel_id=1, source_target_pairs={{0,80},{1,81},{2,82},{3,83},{4,84},{5,85},{6,86},{7,87},{8,88},{9,... | collective-permute-start | bytes 1474568 | tf_op jit(solution)/shard_map/ppermute | solution.py:30
  65.2 1.2 %shard_map.57.own = f32[80,3072]{1,0:T(8,128)S(1)} custom-call(bf16[64,3840]{1,0:T(8,128)(2,1)S(1)} %bitcast.6, bf16[3072,384]{1,0:T(8,128)(2,1)S(1)} %get-tuple-element.18.w_input, f32[384]{0:T(512)S(1)} %get-tuple-element.19.b_input, bf16[384,3072]{1,0:T(8,128)(2,1)S(1)} %get-tuple-element.20.w_output), custom_call_target="tpu_custom_call" | custom-call | flops 377487360 | bytes 5211648 | tf_op jit(solution)/shard_map/pallas_call | solution.py:177
  66.3 0.0 copy-start.1
  66.3 9.9 %collective-permute-done.3.two = bf16[64,3840]{1,0:T(8,128)(2,1)S(1)} collective-permute-done((bf16[64,3840]{1,0:T(8,128)(2,1)S(1)}, bf16[64,3840]{1,0:T(8,128)(2,1)S(1)}, u32[]{:S(2)}, u32[]{:S(2)}) %collective-permute-start.3) | collective-permute-done | bytes 491552 | tf_op jit(solution)/shard_map/ppermute | solution.py:30
  76.2 0.0 collective-permute-done.1.one
  76.2 0.3 shard_map.60.own
  76.5 1.8 %collective-permute-done.5.far = bf16[64,3840]{1,0:T(8,128)(2,1)S(1)} collective-permute-done((bf16[64,3840]{1,0:T(8,128)(2,1)S(1)}, bf16[64,3840]{1,0:T(8,128)(2,1)S(1)}, u32[]{:S(2)}, u32[]{:S(2)}) %collective-permute-start.5) | collective-permute-done | bytes 491552 | tf_op jit(solution)/shard_map/ppermute | solution.py:30
  78.4 0.7 shard_map.62
  79.1 16.9 %all_to_all.11 = bf16[8,8,3840]{2,1,0:T(8,128)(2,1)S(1)} all-to-all(bf16[8,8,3840]{2,1,0:T(8,128)(2,1)S(1)} %bitcast.9), channel_id=1, replica_groups=mesh['x'=4,'y_hi'=2,'core'=2,'y_lo'=4,'z'=8] {'z'}, dimensions={0} | all-to-all | bytes 983040 | tf_op jit(solution)/shard_map/all_to_all | solution.py:34
  96.0 0.9 shard_map.63
  (3 shorter events, 0.0 us)
Async XLA Ops:
  0.0 0.9 copy-start
  27.8 15.3 %collective-permute-start = (bf16[64,3840]{1,0:T(8,128)(2,1)S(1)}, bf16[64,3840]{1,0:T(8,128)(2,1)S(1)}, u32[]{:S(2)}, u32[]{:S(2)}) collective-permute-start(bf16[64,3840]{1,0:T(8,128)(2,1)S(1)} %bitcast.4), channel_id=1, source_target_pairs={{0,8},{1,9},{2,10},{3,11},{4,12},{5,13},{6,14},{7,15},{8,16},{9,17... | collective-permute-start | bytes 1474568 | tf_op jit(solution)/shard_map/ppermute | solution.py:30
  31.3 21.3 %collective-permute-start.2 = (bf16[64,3840]{1,0:T(8,128)(2,1)S(1)}, bf16[64,3840]{1,0:T(8,128)(2,1)S(1)}, u32[]{:S(2)}, u32[]{:S(2)}) collective-permute-start(bf16[64,3840]{1,0:T(8,128)(2,1)S(1)} %bitcast.5), channel_id=1, source_target_pairs={{0,88},{1,89},{2,90},{3,91},{4,92},{5,93},{6,94},{7,95},{8,0},{9,1... | collective-permute-start | bytes 1474568 | tf_op jit(solution)/shard_map/ppermute | solution.py:30
  43.2 18.4 %collective-permute-start.4 = (bf16[64,3840]{1,0:T(8,128)(2,1)S(1)}, bf16[64,3840]{1,0:T(8,128)(2,1)S(1)}, u32[]{:S(2)}, u32[]{:S(2)}) collective-permute-start(bf16[64,3840]{1,0:T(8,128)(2,1)S(1)} %collective-permute-done.packed), channel_id=1, source_target_pairs={{0,8},{1,9},{2,10},{3,11},{4,12},{5,13},{6,14},{7,15},{8,16},{9,17... | collective-permute-start | bytes 1474568 | tf_op jit(solution)/shard_map/ppermute | solution.py:30
  48.0 28.3 %collective-permute-start.1 = (bf16[64,3840]{1,0:T(8,128)(2,1)S(1)}, bf16[64,3840]{1,0:T(8,128)(2,1)S(1)}, u32[]{:S(2)}, u32[]{:S(2)}) collective-permute-start(bf16[64,3840]{1,0:T(8,128)(2,1)S(1)} %shard_map.58), channel_id=1, source_target_pairs={{0,88},{1,89},{2,90},{3,91},{4,92},{5,93},{6,94},{7,95},{8,0},{9,1... | collective-permute-start | bytes 1474568 | tf_op jit(solution)/shard_map/ppermute | solution.py:30
  54.3 22.0 %collective-permute-start.3 = (bf16[64,3840]{1,0:T(8,128)(2,1)S(1)}, bf16[64,3840]{1,0:T(8,128)(2,1)S(1)}, u32[]{:S(2)}, u32[]{:S(2)}) collective-permute-start(bf16[64,3840]{1,0:T(8,128)(2,1)S(1)} %shard_map.59), channel_id=1, source_target_pairs={{0,8},{1,9},{2,10},{3,11},{4,12},{5,13},{6,14},{7,15},{8,16},{9,17... | collective-permute-start | bytes 1474568 | tf_op jit(solution)/shard_map/ppermute | solution.py:30
  63.2 15.2 %collective-permute-start.5 = (bf16[64,3840]{1,0:T(8,128)(2,1)S(1)}, bf16[64,3840]{1,0:T(8,128)(2,1)S(1)}, u32[]{:S(2)}, u32[]{:S(2)}) collective-permute-start(bf16[64,3840]{1,0:T(8,128)(2,1)S(1)} %shard_map.61), channel_id=1, source_target_pairs={{0,80},{1,81},{2,82},{3,83},{4,84},{5,85},{6,86},{7,87},{8,88},{9,... | collective-permute-start | bytes 1474568 | tf_op jit(solution)/shard_map/ppermute | solution.py:30
  66.3 29.7 %copy-start.1 = (f32[3072]{0:T(1024)S(1)}, f32[3072]{0:T(1024)}, u32[]{:S(2)}) copy-start(f32[3072]{0:T(1024)} %b_output.1) | copy-start | bytes 36868

commit v7 on v4

--- a/solution.py
+++ b/solution.py
@@ -90,6 +90,12 @@
         out[:, at] = sums[:MAIN].astype(jnp.bfloat16)
         left = left + dot(puts(q), sums[MAIN:].astype(jnp.bfloat16))
     out[:, features:] = left.astype(jnp.bfloat16)
+
+
+def far_kernel(packed, w_input, b_input, w_output, earlier, low, high, block, out):
+    away_kernel(packed, w_input, b_input, w_output, earlier, out, block)
+    low[...] = out[: MAIN // 2]
+    high[...] = out[MAIN // 2 :]
 
 
 def own_kernel(packed, w_input, b_input, w_output, out, w_input_near, b_input_near, w_output_near, block, arrived):
@@ -120,9 +126,11 @@
         out[:, at] = dot(hidden, w_output_near[:, at])
 
 
-def add_kernel(own, one, two, three, total, packed):
+def add_kernel(own, one, two, low, high, total, packed, three):
     features = own.shape[1]
     part = features // QUARTERS
+    three[: MAIN // 2] = low[...]
+    three[MAIN // 2 :] = high[...]
     terms = (one, two, three)
     main = own[:MAIN]
     for term in terms:
@@ -200,10 +208,13 @@
     up2 = along_y(up1, 1)
     down1 = along_y(mine, -1)
     back = []
-    for away, k in ((up1, -1), (down1, 1), (up2, -2)):
+    for away, k in ((up1, -1), (down1, 1)):
         (part,) = call(away_kernel, (packed,), (away,) + weights, block, flops, (own,))
         back.append(along_y(part, k))
-    total, outgoing = call(add_kernel, (sums, packed), (own, *back))
+    half = jax.ShapeDtypeStruct((MAIN // 2, wide), jnp.bfloat16)
+    low, high = call(far_kernel, (half, half), (up2,) + weights, block + (pltpu.VMEM(packed.shape, packed.dtype),), flops, (own,))
+    back += [along_y(low, -2), along_y(high, -2)]
+    total, outgoing = call(add_kernel, (sums, packed), (own, *back), (pltpu.VMEM(packed.shape, packed.dtype),))
     got = exchange_z(outgoing)
     (out,) = call(
         last_kernel,

time: 97.4 us -> 97.8 us (level)
  starting transfers between devices: 18.9 us -> 24.3 us
  waiting for transfers between devices: 23.4 us -> 18.5 us
    ppermute x6 -> x7, starting transfers between devices: 18.9 us -> 24.3 us  [along_y(): lax.ppermute(block, NAMES, pairs(lambda x, y, c, z: (x, y + k * (1 - 2 *...]
    ppermute x6 -> x7, waiting for transfers between devices: 23.4 us -> 18.5 us  [along_y(): lax.ppermute(block, NAMES, pairs(lambda x, y, c, z: (x, y + k * (1 - 2 *...]
  transfers between devices with their start and end apart: 6 -> 7, of which waited for: 4 -> 4; matrix products, arithmetic and copies ran while one was open for 0% -> 0% of each run, Pallas kernels for 8% -> 8%
where the time goes in v7:
time: 97.8 us; the launch traced here: 97 us
  blocking collectives  43.6 us (45%)
  starting transfers between devices  24.3 us (25%)
  waiting for transfers between devices  18.5 us (19%)
  Pallas kernels  9.63 us (10%)
    all_to_all x2, blocking collectives, exchange_z(): lax.all_to_all(blocks.reshape(Z, EIGHT, -1), 'z', 0, 0, tiled=True)  43.6 us
    ppermute x7, starting transfers between devices, along_y(): lax.ppermute(block, NAMES, pairs(lambda x, y, c, z: (x, y + k * (1 - 2 *...  24.3 us
    ppermute x7, waiting for transfers between devices, along_y(): lax.ppermute(block, NAMES, pairs(lambda x, y, c, z: (x, y + k * (1 - 2 *...  18.5 us
    pallas_call x7, Pallas kernels, call(): pl.pallas_call(kernel, out_shape=outs, in_specs=[pl.BlockSpec(memory_spac...  9.63 us
  transfers between devices with their start and end apart: 7, of which 4 were waited for; matrix products, arithmetic and copies ran while one was open for 0% of the time, Pallas kernels for 8%

profile of v7, /device:TPU:6, one launch (start us, length us, event | category | flops | bytes accessed | tf_op | source)
XLA Modules:
  0.0 97.0 jit_solution(3460469948099443245)
XLA Ops:
  0.0 0.9 copy-done
  0.9 26.9 %all_to_all.10 = bf16[8,8,3840]{2,1,0:T(8,128)(2,1)S(1)} all-to-all(bf16[8,8,3840]{2,1,0:T(8,128)(2,1)S(1)} %bitcast.8), channel_id=1, replica_groups=mesh['x'=4,'y_hi'=2,'core'=2,'y_lo'=4,'z'=8] {'z'}, dimensions={0} | all-to-all | bytes 983040 | tf_op jit(solution)/shard_map/all_to_all | solution.py:34
  27.8 3.5 %collective-permute-start = (bf16[64,3840]{1,0:T(8,128)(2,1)S(1)}, bf16[64,3840]{1,0:T(8,128)(2,1)S(1)}, u32[]{:S(2)}, u32[]{:S(2)}) collective-permute-start(bf16[64,3840]{1,0:T(8,128)(2,1)S(1)} %bitcast.4), channel_id=1, source_target_pairs={{0,8},{1,9},{2,10},{3,11},{4,12},{5,13},{6,14},{7,15},{8,16},{9,17... | collective-permute-start | bytes 1474568 | tf_op jit(solution)/shard_map/ppermute | solution.py:30
  31.3 3.8 %collective-permute-start.2 = (bf16[64,3840]{1,0:T(8,128)(2,1)S(1)}, bf16[64,3840]{1,0:T(8,128)(2,1)S(1)}, u32[]{:S(2)}, u32[]{:S(2)}) collective-permute-start(bf16[64,3840]{1,0:T(8,128)(2,1)S(1)} %bitcast.5), channel_id=1, source_target_pairs={{0,88},{1,89},{2,90},{3,91},{4,92},{5,93},{6,94},{7,95},{8,0},{9,1... | collective-permute-start | bytes 1474568 | tf_op jit(solution)/shard_map/ppermute | solution.py:30
  35.1 3.0 %shard_map.56 = (f32[80,3072]{1,0:T(8,128)S(1)}, bf16[3072,384]{1,0:T(8,128)(2,1)S(1)}, f32[384]{0:T(512)S(1)}, bf16[384,3072]{1,0:T(8,128)(2,1)S(1)}) custom-call(bf16[64,3840]{1,0:T(8,128)(2,1)S(1)} %bitcast.6, bf16[3072,384]{1,0:T(8,128)(2,1)} %w_input.1, f32[384]{0:T(512)} %b_input.1, bf16[384,3072]{1,0:T(8,128)(2,1)} %w_output.1), custom_call_target="tpu_custom_call" | custom-call | flops 377487360 | bytes 5211648 | tf_op jit(solution)/shard_map/pallas_call | solution.py:173
  38.1 5.0 %collective-permute-done.packed = bf16[64,3840]{1,0:T(8,128)(2,1)S(1)} collective-permute-done((bf16[64,3840]{1,0:T(8,128)(2,1)S(1)}, bf16[64,3840]{1,0:T(8,128)(2,1)S(1)}, u32[]{:S(2)}, u32[]{:S(2)}) %collective-permute-start) | collective-permute-done | bytes 491552 | tf_op jit(solution)/shard_map/ppermute | solution.py:30
  43.2 3.1 %collective-permute-start.4 = (bf16[64,3840]{1,0:T(8,128)(2,1)S(1)}, bf16[64,3840]{1,0:T(8,128)(2,1)S(1)}, u32[]{:S(2)}, u32[]{:S(2)}) collective-permute-start(bf16[64,3840]{1,0:T(8,128)(2,1)S(1)} %collective-permute-done.packed), channel_id=1, source_target_pairs={{0,8},{1,9},{2,10},{3,11},{4,12},{5,13},{6,14},{7,15},{8,16},{9,17... | collective-permute-start | bytes 1474568 | tf_op jit(solution)/shard_map/ppermute | solution.py:30
  46.3 1.7 %shard_map.57 = bf16[64,3840]{1,0:T(8,128)(2,1)S(1)} custom-call(bf16[64,3840]{1,0:T(8,128)(2,1)S(1)} %collective-permute-done.packed, bf16[3072,384]{1,0:T(8,128)(2,1)S(1)} %get-tuple-element.18.w_input, f32[384]{0:T(512)S(1)} %get-tuple-element.19.b_input, bf16[384,3072]{1,0:T(8,128)(2,1)S(1)} %get-tuple-element.20.w_output, ...), custom_call_target="tpu_custom_call" | custom-call | flops 377487360 | bytes 5211648 | tf_op jit(solution)/shard_map/pallas_call | solution.py:173
  48.0 4.6 %collective-permute-start.1 = (bf16[64,3840]{1,0:T(8,128)(2,1)S(1)}, bf16[64,3840]{1,0:T(8,128)(2,1)S(1)}, u32[]{:S(2)}, u32[]{:S(2)}) collective-permute-start(bf16[64,3840]{1,0:T(8,128)(2,1)S(1)} %shard_map.57), channel_id=1, source_target_pairs={{0,88},{1,89},{2,90},{3,91},{4,92},{5,93},{6,94},{7,95},{8,0},{9,1... | collective-permute-start | bytes 1474568 | tf_op jit(solution)/shard_map/ppermute | solution.py:30
  52.6 0.0 collective-permute-done.2.packed
  52.6 1.7 %shard_map.58 = bf16[64,3840]{1,0:T(8,128)(2,1)S(1)} custom-call(bf16[64,3840]{1,0:T(8,128)(2,1)S(1)} %collective-permute-done.2.packed, bf16[3072,384]{1,0:T(8,128)(2,1)S(1)} %get-tuple-element.18.w_input, f32[384]{0:T(512)S(1)} %get-tuple-element.19.b_input, bf16[384,3072]{1,0:T(8,128)(2,1)S(1)} %get-tuple-element.20.w_output, ...), custom_call_target="tpu_custom_call" | custom-call | flops 377487360 | bytes 5211648 | tf_op jit(solution)/shard_map/pallas_call | solution.py:173
  54.3 1.9 %collective-permute-start.3 = (bf16[64,3840]{1,0:T(8,128)(2,1)S(1)}, bf16[64,3840]{1,0:T(8,128)(2,1)S(1)}, u32[]{:S(2)}, u32[]{:S(2)}) collective-permute-start(bf16[64,3840]{1,0:T(8,128)(2,1)S(1)} %shard_map.58), channel_id=1, source_target_pairs={{0,8},{1,9},{2,10},{3,11},{4,12},{5,13},{6,14},{7,15},{8,16},{9,17... | collective-permute-start | bytes 1474568 | tf_op jit(solution)/shard_map/ppermute | solution.py:30
  56.2 5.4 %collective-permute-done.4.packed = bf16[64,3840]{1,0:T(8,128)(2,1)S(1)} collective-permute-done((bf16[64,3840]{1,0:T(8,128)(2,1)S(1)}, bf16[64,3840]{1,0:T(8,128)(2,1)S(1)}, u32[]{:S(2)}, u32[]{:S(2)}) %collective-permute-start.4) | collective-permute-done | bytes 491552 | tf_op jit(solution)/shard_map/ppermute | solution.py:30
  61.6 1.7 %shard_map.59 = (bf16[32,3840]{1,0:T(8,128)(2,1)S(1)}, bf16[32,3840]{1,0:T(8,128)(2,1)S(1)}) custom-call(bf16[64,3840]{1,0:T(8,128)(2,1)S(1)} %collective-permute-done.4.packed, bf16[3072,384]{1,0:T(8,128)(2,1)S(1)} %get-tuple-element.18.w_input, f32[384]{0:T(512)S(1)} %get-tuple-element.19.b_input, bf16[384,3072]{1,0:T(8,128)(2,1)S(1)} %get-tuple-element.20.w_output, ...), custom_call_target="tpu_custom_call" | custom-call | flops 377487360 | bytes 5211648 | tf_op jit(solution)/shard_map/pallas_call | solution.py:173
  63.2 0.0 copy-start.1
  63.3 1.9 %collective-permute-start.5 = (bf16[32,3840]{1,0:T(8,128)(2,1)S(1)}, bf16[32,3840]{1,0:T(8,128)(2,1)S(1)}, u32[]{:S(2)}, u32[]{:S(2)}) collective-permute-start(bf16[32,3840]{1,0:T(8,128)(2,1)S(1)} %get-tuple-element.21), channel_id=1, source_target_pairs={{0,80},{1,81},{2,82},{3,83},{4,84},{5,85},{6,86},{7,87},{8,88},{9,... | collective-permute-start | bytes 737288 | tf_op jit(solution)/shard_map/ppermute | solution.py:30
  65.2 5.4 %collective-permute-start.6 = (bf16[32,3840]{1,0:T(8,128)(2,1)S(1)}, bf16[32,3840]{1,0:T(8,128)(2,1)S(1)}, u32[]{:S(2)}, u32[]{:S(2)}) collective-permute-start(bf16[32,3840]{1,0:T(8,128)(2,1)S(1)} %get-tuple-element.22), channel_id=1, source_target_pairs={{0,80},{1,81},{2,82},{3,83},{4,84},{5,85},{6,86},{7,87},{8,88},{9,... | collective-permute-start | bytes 737288 | tf_op jit(solution)/shard_map/ppermute | solution.py:30
  70.6 0.0 collective-permute-done.1.one
  70.6 5.7 %collective-permute-done.3.two = bf16[64,3840]{1,0:T(8,128)(2,1)S(1)} collective-permute-done((bf16[64,3840]{1,0:T(8,128)(2,1)S(1)}, bf16[64,3840]{1,0:T(8,128)(2,1)S(1)}, u32[]{:S(2)}, u32[]{:S(2)}) %collective-permute-start.3) | collective-permute-done | bytes 491552 | tf_op jit(solution)/shard_map/ppermute | solution.py:30
  76.3 0.0 collective-permute-done.5.low
  76.3 2.4 %collective-permute-done.6.high = bf16[32,3840]{1,0:T(8,128)(2,1)S(1)} collective-permute-done((bf16[32,3840]{1,0:T(8,128)(2,1)S(1)}, bf16[32,3840]{1,0:T(8,128)(2,1)S(1)}, u32[]{:S(2)}, u32[]{:S(2)}) %collective-permute-start.6) | collective-permute-done | bytes 245792 | tf_op jit(solution)/shard_map/ppermute | solution.py:30
  78.6 0.8 shard_map.60
  79.4 16.7 %all_to_all.11 = bf16[8,8,3840]{2,1,0:T(8,128)(2,1)S(1)} all-to-all(bf16[8,8,3840]{2,1,0:T(8,128)(2,1)S(1)} %bitcast.9), channel_id=1, replica_groups=mesh['x'=4,'y_hi'=2,'core'=2,'y_lo'=4,'z'=8] {'z'}, dimensions={0} | all-to-all | bytes 983040 | tf_op jit(solution)/shard_map/all_to_all | solution.py:34
  96.1 0.9 shard_map.61
  (3 shorter events, 0.0 us)
Async XLA Ops:
  0.0 0.9 copy-start
  27.8 15.3 %collective-permute-start = (bf16[64,3840]{1,0:T(8,128)(2,1)S(1)}, bf16[64,3840]{1,0:T(8,128)(2,1)S(1)}, u32[]{:S(2)}, u32[]{:S(2)}) collective-permute-start(bf16[64,3840]{1,0:T(8,128)(2,1)S(1)} %bitcast.4), channel_id=1, source_target_pairs={{0,8},{1,9},{2,10},{3,11},{4,12},{5,13},{6,14},{7,15},{8,16},{9,17... | collective-permute-start | bytes 1474568 | tf_op jit(solution)/shard_map/ppermute | solution.py:30
  31.3 21.3 %collective-permute-start.2 = (bf16[64,3840]{1,0:T(8,128)(2,1)S(1)}, bf16[64,3840]{1,0:T(8,128)(2,1)S(1)}, u32[]{:S(2)}, u32[]{:S(2)}) collective-permute-start(bf16[64,3840]{1,0:T(8,128)(2,1)S(1)} %bitcast.5), channel_id=1, source_target_pairs={{0,88},{1,89},{2,90},{3,91},{4,92},{5,93},{6,94},{7,95},{8,0},{9,1... | collective-permute-start | bytes 1474568 | tf_op jit(solution)/shard_map/ppermute | solution.py:30
  43.2 18.4 %collective-permute-start.4 = (bf16[64,3840]{1,0:T(8,128)(2,1)S(1)}, bf16[64,3840]{1,0:T(8,128)(2,1)S(1)}, u32[]{:S(2)}, u32[]{:S(2)}) collective-permute-start(bf16[64,3840]{1,0:T(8,128)(2,1)S(1)} %collective-permute-done.packed), channel_id=1, source_target_pairs={{0,8},{1,9},{2,10},{3,11},{4,12},{5,13},{6,14},{7,15},{8,16},{9,17... | collective-permute-start | bytes 1474568 | tf_op jit(solution)/shard_map/ppermute | solution.py:30
  48.0 22.6 %collective-permute-start.1 = (bf16[64,3840]{1,0:T(8,128)(2,1)S(1)}, bf16[64,3840]{1,0:T(8,128)(2,1)S(1)}, u32[]{:S(2)}, u32[]{:S(2)}) collective-permute-start(bf16[64,3840]{1,0:T(8,128)(2,1)S(1)} %shard_map.57), channel_id=1, source_target_pairs={{0,88},{1,89},{2,90},{3,91},{4,92},{5,93},{6,94},{7,95},{8,0},{9,1... | collective-permute-start | bytes 1474568 | tf_op jit(solution)/shard_map/ppermute | solution.py:30
  54.3 21.9 %collective-permute-start.3 = (bf16[64,3840]{1,0:T(8,128)(2,1)S(1)}, bf16[64,3840]{1,0:T(8,128)(2,1)S(1)}, u32[]{:S(2)}, u32[]{:S(2)}) collective-permute-start(bf16[64,3840]{1,0:T(8,128)(2,1)S(1)} %shard_map.58), channel_id=1, source_target_pairs={{0,8},{1,9},{2,10},{3,11},{4,12},{5,13},{6,14},{7,15},{8,16},{9,17... | collective-permute-start | bytes 1474568 | tf_op jit(solution)/shard_map/ppermute | solution.py:30
  63.2 32.9 %copy-start.1 = (f32[3072]{0:T(1024)S(1)}, f32[3072]{0:T(1024)}, u32[]{:S(2)}) copy-start(f32[3072]{0:T(1024)} %b_output.1) | copy-start | bytes 36868
  63.3 13.0 %collective-permute-start.5 = (bf16[32,3840]{1,0:T(8,128)(2,1)S(1)}, bf16[32,3840]{1,0:T(8,128)(2,1)S(1)}, u32[]{:S(2)}, u32[]{:S(2)}) collective-permute-start(bf16[32,3840]{1,0:T(8,128)(2,1)S(1)} %get-tuple-element.21), channel_id=1, source_target_pairs={{0,80},{1,81},{2,82},{3,83},{4,84},{5,85},{6,86},{7,87},{8,88},{9,... | collective-permute-start | bytes 737288 | tf_op jit(solution)/shard_map/ppermute | solution.py:30
  65.2 13.4 %collective-permute-start.6 = (bf16[32,3840]{1,0:T(8,128)(2,1)S(1)}, bf16[32,3840]{1,0:T(8,128)(2,1)S(1)}, u32[]{:S(2)}, u32[]{:S(2)}) collective-permute-start(bf16[32,3840]{1,0:T(8,128)(2,1)S(1)} %get-tuple-element.22), channel_id=1, source_target_pairs={{0,80},{1,81},{2,82},{3,83},{4,84},{5,85},{6,86},{7,87},{8,88},{9,... | collective-permute-start | bytes 737288 | tf_op jit(solution)/shard_map/ppermute | solution.py:30
